TPU v7x, 128 devices: a whole 4x4x4 slice. The times are simulated.
128 devices in a mesh: dp: 2 (over y_hi), blk: 8 (over x, core), heads: 8 (over y_lo, z).
Axes of the slice: x: 4, y: 4 (y_hi: 2, y_lo: 2; y = y_hi * 2 + y_lo), z: 4, core: 2. Of those that a mesh axis runs over, the one named last changes fastest.
Arguments:
- tokens: bfloat16 [2, 8192, 4096], P('dp', ('blk', 'heads')), may hold values from -24 to 24
- norm_gain: float32 [4096], replicated, may hold values from 0.5 to 1.5
- segment_ids: int32 [2, 8192], P('dp', ('blk', 'heads')), may hold values from 0 to 7, never falling along the last dimension, each value on 1 to 4096 neighbouring positions
- w_query: bfloat16 [4096, 4096], P(None, 'heads'), may hold values from -2 to 2
- w_key: bfloat16 [4096, 1024], P(None, 'heads'), may hold values from -2 to 2
- w_value: bfloat16 [4096, 1024], P(None, 'heads'), may hold values from -0.09375 to 0.09375
- w_out: bfloat16 [4096, 4096], P('heads'), may hold values from -1 to 1
Outputs:
- attn_delta: bfloat16 [2, 8192, 4096], P('dp', ('blk', 'heads'))
- input_gram: float32 [4096, 4096], P(('dp', 'blk', 'heads'))
Inputs may be any that keep to these rules, and one draw needn't show every extreme that they name: `segment_ids`: segment numbers never fall along a sequence; a document holds at most 4096 positions, and one holds exactly that many.
All inputs are finite; a program needn't handle non-finite values.
Results may differ from a plain program's by a relative error of at most 0.02.
Values may be sent and summed in bfloat16 or wider, within the bound.
A program may use at most 128 MiB of HBM per device.

v0:
```python
import math

import jax
import jax.numpy as jnp
from jax import lax
from jax.sharding import PartitionSpec as P

HD = 128


EPSILON = 1e-05
ROPE_BASE = 500000.0
NEGATIVE = -1e30
KEY_STEP = 1024


def rotate(values, positions):
    head_width = values.shape[-1]
    half_width = head_width // 2
    frequency = ROPE_BASE ** (-(jnp.arange(half_width, dtype=jnp.float32) * 2.0 / head_width))
    angles = positions[:, None] * frequency[None, :]
    cosine = jnp.cos(angles)[:, None, :]
    sine_part = jnp.sin(angles)[:, None, :]
    lower_half = values[..., :half_width]
    upper_half = values[..., half_width:]
    return jnp.concatenate(
        [
            lower_half * cosine - upper_half * sine_part,
            upper_half * cosine + lower_half * sine_part,
        ],
        -1,
    )


def per_device(tokens, norm_gain, segment_ids, w_query, w_key, w_value, w_out):
    local_rows = tokens.shape[1]
    model_width = tokens.shape[2]
    inputs = tokens[0].astype(jnp.float32)
    mean_square = jnp.mean(inputs * inputs, axis=-1, keepdims=True)
    normed = (inputs * lax.rsqrt(mean_square + EPSILON) * norm_gain).astype(jnp.bfloat16)
    span_dp = lax.axis_size("dp")
    span_blk = lax.axis_size("blk")
    span_heads = lax.axis_size("heads")
    head_index = lax.axis_index("heads")
    row_share = model_width // (span_dp * span_blk * span_heads)
    block_rows = local_rows * span_heads
    query_width = w_query.shape[1]
    key_width = w_key.shape[1]
    seg_buffer = jnp.zeros((block_rows,), jnp.int32)
    shard_rows = lax.all_gather(normed, "heads", axis=0, tiled=True)
    seg_piece = lax.all_gather(segment_ids[0], "heads", axis=0, tiled=True)
    seg_buffer = lax.dynamic_update_slice_in_dim(seg_buffer, seg_piece, jnp.int32(0), 0)
    seg_ids = seg_buffer
    row_count = shard_rows.shape[0]
    split_view = shard_rows.reshape(row_count, span_dp, span_blk, span_heads, row_share)
    picked = lax.dynamic_index_in_dim(split_view, head_index, 3, keepdims=False)
    gram_part = lax.dot_general(
        picked.reshape(row_count, span_dp * span_blk * row_share),
        shard_rows,
        (((0,), (0,)), ((), ())),
        preferred_element_type=jnp.float32,
    )
    q_proj = jnp.dot(shard_rows, w_query, preferred_element_type=jnp.float32)
    key_proj = jnp.dot(shard_rows, w_key, preferred_element_type=jnp.float32)
    val_proj = jnp.dot(shard_rows, w_value, preferred_element_type=jnp.float32)
    first_row = lax.axis_index("blk") * block_rows
    position_ids = first_row + jnp.arange(block_rows, dtype=jnp.int32)
    positions = position_ids.astype(jnp.float32)
    query_heads = query_width // HD
    kv_heads = key_width // HD
    group_size = query_heads // kv_heads
    queries = (
        rotate(q_proj.reshape(block_rows, query_heads, HD), positions)
        .astype(jnp.bfloat16)
        .reshape(block_rows, kv_heads, group_size, HD)
    )
    key_rot = (
        rotate(key_proj.reshape(block_rows, kv_heads, HD), positions)
        .astype(jnp.bfloat16)
        .reshape(block_rows, key_width)
    )
    val_rows = val_proj.astype(jnp.bfloat16)
    score_scale = 1.0 / math.sqrt(HD)
    last_position = first_row + block_rows - 1
    first_segment = seg_ids[0]

    def attend(carried, key_part, val_part, seg_part, key_anchor):
        running_max, denom_sum, weighted = carried
        row_count = key_part.shape[0]
        scores = (
            jnp.einsum(
                "rkgd,skd->kgrs",
                queries,
                key_part.reshape(row_count, kv_heads, HD),
                preferred_element_type=jnp.float32,
            )
            * score_scale
        )
        key_pos = key_anchor + jnp.arange(row_count, dtype=jnp.int32)
        allowed = (seg_part[None, :] == seg_ids[:, None]) & (
            key_pos[None, :] <= position_ids[:, None]
        )
        scores = jnp.where(allowed, scores, NEGATIVE)
        new_max = jnp.maximum(running_max, jnp.max(scores, axis=-1))
        exponent = jnp.where(allowed, jnp.exp(scores - new_max[..., None]), 0.0)
        rescale = jnp.exp(running_max - new_max)
        denom_sum = denom_sum * rescale + jnp.sum(exponent, axis=-1)
        weighted = weighted * rescale[..., None] + jnp.einsum(
            "kgrs,skd->kgrd",
            exponent.astype(jnp.bfloat16),
            val_part.reshape(row_count, kv_heads, HD),
            preferred_element_type=jnp.float32,
        )
        return (new_max, denom_sum, weighted)

    state_shape = (kv_heads, group_size, block_rows)
    cycle_start = (
        jnp.full(state_shape, NEGATIVE, jnp.float32),
        jnp.zeros(state_shape, jnp.float32),
        jnp.zeros(state_shape + (HD,), jnp.float32),
    )
    carried = cycle_start
    anchor = jnp.int32(0)
    key_all = lax.all_gather(key_rot, "blk", axis=0, tiled=True)
    val_all = lax.all_gather(val_rows, "blk", axis=0, tiled=True)
    seg_all = lax.all_gather(seg_ids, "blk", axis=0, tiled=True)
    step_rows = math.gcd(KEY_STEP, key_all.shape[0])
    for block_number in range(key_all.shape[0] // step_rows):
        low_row = block_number * step_rows
        key_part = key_all[low_row : low_row + step_rows]
        val_part = val_all[low_row : low_row + step_rows]
        seg_part = seg_all[low_row : low_row + step_rows]
        key_anchor = anchor + low_row
        needed = (key_anchor <= last_position) & (seg_part[step_rows - 1] >= first_segment)
        carried = lax.cond(
            needed,
            lambda state_now: attend(state_now, key_part, val_part, seg_part, key_anchor),
            lambda state_now: state_now,
            carried,
        )
    running_max, denom_sum, weighted = carried
    attended = (weighted / denom_sum[..., None]).astype(jnp.bfloat16)
    attended = attended.transpose(2, 0, 1, 3).reshape(block_rows, query_width)
    delta_sum = lax.psum_scatter(
        jnp.dot(attended, w_out, preferred_element_type=jnp.float32).astype(jnp.bfloat16),
        "heads",
        scatter_dimension=0,
        tiled=True,
    )
    gram_rows = lax.psum_scatter(
        gram_part.astype(jnp.bfloat16), ("dp", "blk"), scatter_dimension=0, tiled=True
    ).astype(jnp.float32)
    total_rows = block_rows * span_blk * span_dp
    input_gram = gram_rows / total_rows
    return (delta_sum[None], input_gram)


def solution(mesh):
    return jax.shard_map(
        per_device,
        mesh=mesh,
        in_specs=(
            P("dp", ("blk", "heads"), None),
            P(),
            P("dp", ("blk", "heads")),
            P(None, "heads"),
            P(None, "heads"),
            P(None, "heads"),
            P("heads", None),
        ),
        out_specs=(P("dp", ("blk", "heads"), None), P(("dp", "blk", "heads"), None)),
        check_vma=False,
    )
```

profile of v0, /device:TPU:1, one launch (start us, length us, event | category | flops | bytes accessed | tf_op | source)
XLA Modules:
  0.0 405.4 jit_solution(5378660091945852600)
XLA Ops:
  7.2 1.8 copy.35
  9.6 2.2 fusion.140
  11.9 98.7 %all-gather.6.cloned.1.call-done = bf16[1024,4096]{0,1:T(8,128)(2,1)} async-done(((bf16[128,4096]{0,1:T(8,128)(2,1)}), bf16[1024,4096]{0,1:T(8,128)(2,1)}) %all-gather.6.cloned.1.call-update) | async-done | bytes 8388624 | tf_op jit(solution)/shard_map/all_gather | solution.py:50
  110.5 4.7 %convolution_bitcast_fusion = f32[1024,1,128]{0,2,1:T(8,128)S(1)} fusion(bf16[1024,4096]{0,1:T(8,128)(2,1)} %all-gather.6.cloned.1.call-done, bf16[4096,128]{1,0:T(8,128)(2,1)S(1)} %copy-done), kind=kOutput, calls=%fused_computation.189 | convolution fusion | flops 1073741824 | bytes 9961472 | tf_op jit(solution)/shard_map/dot_general | solution.py:64
  115.3 1.2 fusion.152
  117.2 6.5 %convolution_convert_fusion.2 = bf16[1024,128]{1,0:T(8,128)(2,1)} fusion(bf16[1024,4096]{0,1:T(8,128)(2,1)} %all-gather.6.cloned.1.call-done, bf16[4096,128]{1,0:T(8,128)(2,1)S(1)} %copy-done.7), kind=kOutput, calls=%fused_computation.190 | convolution fusion | flops 1073872896 | bytes 9699328 | tf_op jit(solution)/shard_map/dot_general | solution.py:65
  123.8 1.3 constant_dynamic-slice_fusion
  125.1 9.5 %convolution_convert_fusion.1 = bf16[512,4096]{1,0:T(8,128)(2,1)} fusion(bf16[1024,512]{0,1:T(8,128)(2,1)S(1)} %bitcast.416, bf16[1024,4096]{0,1:T(8,128)(2,1)} %all-gather.6.cloned.1.call-done), kind=kOutput, calls=%fused_computation.180 | convolution fusion | flops 4297064448 | bytes 13631488 | tf_op jit(solution)/shard_map/dot_general | solution.py:57
  134.7 14.8 %all-gather = s32[1,1024]{1,0:T(1,128)S(1)} all-gather(s32[1,128]{1,0:T(1,128)S(1)} %copy-done.6), channel_id=2, replica_groups=mesh['dp'=2,'blk'=8,'heads'=8] {'heads'}, dimensions={1}, use_global_device_ids=true | all-gather | bytes 4608 | tf_op jit(solution)/shard_map/all_gather | solution.py:51
  150.0 20.1 %all-gather.1 = s32[1,8192]{1,0:T(1,128)S(1)} all-gather(s32[1,1024]{1,0:T(1,128)S(1)} %all-gather), channel_id=3, replica_groups=mesh['dp'=2,'blk'=8,'heads'=8] {'blk'}, dimensions={1}, use_global_device_ids=true | all-gather | bytes 36864 | tf_op jit(solution)/shard_map/all_gather | solution.py:126
  180.2 3.1 multiply_cosine_fusion
  183.2 8.4 %fusion.160 = f32[1024,512]{0,1:T(8,128)S(1)} fusion(bf16[1024,4096]{0,1:T(8,128)(2,1)} %all-gather.6.cloned.1.call-done, bf16[4096,512]{1,0:T(8,128)(2,1)} %param.26), kind=kOutput, calls=%fused_computation.220 | convolution fusion | flops 4294967296 | bytes 14680064 | tf_op jit(solution)/shard_map/dot_general | solution.py:63
  192.7 1.9 copy.70
  194.6 2.0 copy.69
  196.6 2.5 fusion.141
  199.7 1.6 fusion.156
  201.4 2.3 fusion.155
  203.7 15.7 %conditional.8 = (f32[1,4,1024]{2,1,0:T(4,128)S(1)}, f32[1,4,1024]{2,1,0:T(4,128)S(1)}, f32[1,4,1024,128]{3,2,1,0:T(8,128)}) conditional(s32[]{:T(128)} %convert_element_type.98, () %tuple.59, (s32[1024]{0:T(1024)S(1)}, s32[1024]{0:T(1024)S(1)}, s32[1024]{0:T(1024)S(1)}, bf16[1024,1,4,128]{3,0,2,1:T(8,128)(2,1)S(1)}, bf16[1024,128]{0,1:T(8,128)(2,1)S(1)}, ...), branch_computations={%region_1.2_spmd, %region_2.5_spmd} | conditional | flops 2205700096 | bytes 58404888 | solution.py:135
  204.5 4.1 %fusion = (f32[4,1024]{1,0:T(4,128)S(1)}, f32[1024,1024,4]{1,0,2:T(8,128)S(1)}) fusion(pred[1024,1024]{0,1:T(8,128)(4,1)S(1)} %fusion.7, bf16[1024,1,4,128]{3,0,2,1:T(8,128)(2,1)S(1)} %get-tuple-element.188, bf16[1024,128]{0,1:T(8,128)(2,1)S(1)} %get-tuple-element.374), kind=kOutput, calls=%fused_computation.2 | convolution fusion | flops 1086320640 | bytes 19152896 | tf_op jit(solution)/shard_map/cond/branch_1_fun/rkgd,skd->kgrs/dot_general | solution.py:91
  208.7 4.2 %fusion.2 = f32[4,1024]{1,0:T(4,128)S(1)} fusion(f32[1024,1024,4]{1,0,2:T(8,128)S(1)} %get-tuple-element.463, f32[4,1024]{1,0:T(4,128)S(1)} %get-tuple-element.461, pred[1024,1024]{0,1:T(8,128)(4,1)S(1)} %fusion.7), kind=kLoop, calls=%fused_computation.4 | loop fusion | flops 20967424 | bytes 17858560 | tf_op jit(solution)/shard_map/cond/branch_1_fun/reduce_sum | solution.py:107
  212.9 6.5 %add_bitcast_fusion = f32[1,4,1024,128]{3,2,1,0:T(8,128)} fusion(f32[1024,1024,4]{1,0,2:T(8,128)S(1)} %get-tuple-element.463, f32[4,1024]{1,0:T(4,128)S(1)} %get-tuple-element.461, pred[1024,1024]{0,1:T(8,128)(4,1)S(1)} %fusion.7, f32[4,1024]{1,0:T(4,128)S(1)} %get-tuple-element.460, bf16[1024,128]{1,0:T(8,128)(2,1)S(1)} %get-tuple-element.189), kind=kOutput, calls=%fused_computation.10 | convolution fusion | flops 1095237632 | bytes 20217856 | tf_op jit(solution)/shard_map/cond/branch_1_fun/kgrs,skd->kgrd/dot_general | solution.py:108
  219.4 17.3 %conditional.9 = ((f32[1,4,1024]{2,1,0:T(4,128)S(1)}, f32[1,4,1024]{2,1,0:T(4,128)S(1)}, f32[1,4,1024,128]{3,2,1,0:T(8,128)})) conditional(s32[]{:T(128)} %convert_element_type.97, (f32[1,4,1024]{2,1,0:T(4,128)S(1)}, f32[1,4,1024]{2,1,0:T(4,128)S(1)}, f32[1,4,1024,128]{3,2,1,0:T(8,128)}) %conditional.8, (s32[1024]{0:T(1024)S(1)}, s32[1024]{0:T(1024)S(1)}, ...), branch_computations={%region_5.6_spmd, %region_6.9_spmd} | conditional | flops 2206217216 | bytes 61624380 | solution.py:135
  219.6 1.2 compare_and_fusion
  220.8 4.1 %fusion.18 = (f32[4,1024]{1,0:T(4,128)S(1)}, f32[1024,1024,4]{1,0,2:T(8,128)S(1)}) fusion(pred[1024,1024]{0,1:T(8,128)(4,1)S(1)} %compare_and_fusion, bf16[1024,1,4,128]{3,0,2,1:T(8,128)(2,1)S(1)} %get-tuple-element.195, bf16[1024,128]{0,1:T(8,128)(2,1)S(1)} %get-tuple-element.380), kind=kOutput, calls=%fused_computation.24 | convolution fusion | flops 1086320640 | bytes 19152896 | tf_op jit(solution)/shard_map/cond/branch_1_fun/rkgd,skd->kgrs/dot_general | solution.py:91
  225.0 7.5 %bitcast_add_fusion.1 = f32[1,4,1024,128]{3,2,1,0:T(8,128)} fusion(f32[1,4,1024,128]{3,2,1,0:T(8,128)} %get-tuple-element.197, f32[1024,1024,4]{1,0,2:T(8,128)S(1)} %get-tuple-element.465, f32[4,1024]{1,0:T(4,128)S(1)} %bitcast.425, pred[1024,1024]{0,1:T(8,128)(4,1)S(1)} %compare_and_fusion, f32[4,1024]{1,0:T(4,128)S(1)} %get-tuple-element.444, ...), kind=kOutput, calls=%fused_computation.31 | convolution fusion | flops 1095761920 | bytes 22315008 | tf_op jit(solution)/shard_map/cond/branch_1_fun/kgrs,skd->kgrd/dot_general | solution.py:108
  232.4 4.2 %fusion.20 = f32[4,1024]{1,0:T(4,128)S(1)} fusion(f32[1024,1024,4]{1,0,2:T(8,128)S(1)} %get-tuple-element.465, f32[4,1024]{1,0:T(4,128)S(1)} %bitcast.426, pred[1024,1024]{0,1:T(8,128)(4,1)S(1)} %compare_and_fusion), kind=kLoop, calls=%fused_computation.26 | loop fusion | flops 20967424 | bytes 17858560 | tf_op jit(solution)/shard_map/cond/branch_1_fun/reduce_sum | solution.py:107
  238.0 8.0 %conditional.13 = ((f32[1,4,1024]{2,1,0:T(4,128)S(1)}, f32[1,4,1024]{2,1,0:T(4,128)S(1)}, f32[1,4,1024,128]{3,2,1,0:T(8,128)})) conditional(s32[]{:T(128)} %convert_element_type.93, (f32[1,4,1024]{2,1,0:T(4,128)S(1)}, f32[1,4,1024]{2,1,0:T(4,128)S(1)}, f32[1,4,1024,128]{3,2,1,0:T(8,128)}) %get-tuple-element.559, (s32[1024]{0:T(1024)S(1)}, ...), branch_computations={%region_21.22_spmd, %region_22.25_spmd} | conditional | flops 2206217216 | bytes 60575776 | solution.py:135
  246.0 7.0 %conditional.15 = (f32[1,4,1024]{2,1,0:T(4,128)S(1)}, f32[1,4,1024,128]{2,3,1,0:T(8,128)S(1)}) conditional(s32[]{:T(128)} %convert_element_type.91, (f32[1,4,1024]{2,1,0:T(4,128)S(1)}, f32[1,4,1024,128]{3,2,1,0:T(8,128)}) %tuple.67, (s32[8192]{0:T(1024)}, s32[1024]{0:T(1024)S(1)}, s32[1024]{0:T(1024)S(1)}, bf16[8192,128]{0,1:T(8,128)(2,1)}, ...), branch_computations={%region_29.30_spmd, %region_30.33_spmd} | conditional | flops 2206221312 | bytes 68939792 | solution.py:135
  246.0 1.9 copy.67
  253.3 9.1 %convolution_convert_fusion = bf16[1024,4096]{1,0:T(8,128)(2,1)} fusion(bf16[1024,512]{0,1:T(8,128)(2,1)S(1)} %bitcast.415, bf16[512,4096]{1,0:T(8,128)(2,1)} %param.29), kind=kOutput, calls=%fused_computation.179 | convolution fusion | flops 4299161600 | bytes 13631488 | tf_op jit(solution)/shard_map/dot_general | solution.py:145
  262.5 1.8 convert_multiply_fusion.2
  264.2 134.4 %reduce-scatter.3.cloned.1.call-done = bf16[128,4096]{1,0:T(8,128)(2,1)} async-done(((bf16[1024,4096]{1,0:T(8,128)(2,1)}), bf16[128,4096]{1,0:T(8,128)(2,1)}) %reduce-scatter.3.cloned.1.call-update) | async-done | bytes 1048592 | tf_op jit(solution)/shard_map/reduce_scatter | solution.py:144
  (52 shorter events, 7.1 us)
Async XLA Ops:
  7.2 103.4 %copy-start = (bf16[4096,128]{1,0:T(8,128)(2,1)S(1)}, bf16[4096,128]{1,0:T(8,128)(2,1)}, u32[]{:S(2)}) copy-start(bf16[4096,128]{1,0:T(8,128)(2,1)} %param.27) | copy-start | bytes 3145732
  7.2 110.0 %copy-start.7 = (bf16[4096,128]{1,0:T(8,128)(2,1)S(1)}, bf16[4096,128]{1,0:T(8,128)(2,1)}, u32[]{:S(2)}) copy-start(bf16[4096,128]{1,0:T(8,128)(2,1)} %param.28) | copy-start | bytes 3145732
  7.2 103.3 %all-gather.6.cloned.1.call-start = ((), (), s32[]{:S(2)}) async-start(), calls=%async_computation.2 | async-start | bytes 9437184 | tf_op jit(solution)/shard_map/all_gather | solution.py:50
  11.8 188.0 %all-gather.8.cloned.1.call-start = ((), (), s32[]{:S(2)}) async-start(), calls=%async_computation.3 | async-start | bytes 2359296 | tf_op jit(solution)/shard_map/all_gather | solution.py:124
  117.2 84.2 %all-gather.10.cloned.1.call-start = ((), (), s32[]{:S(2)}) async-start(), calls=%async_computation.4 | async-start | bytes 2359296 | tf_op jit(solution)/shard_map/all_gather | solution.py:125
  123.7 138.7 %reduce-scatter.5.cloned.1.call-start = ((), (), s32[]{:S(2)}) async-start(), calls=%async_computation.6 | async-start | bytes 4456448 | tf_op jit(solution)/shard_map/reduce_scatter | solution.py:150
  123.8 10.9 %copy-start.6 = (s32[1,128]{1,0:T(1,128)S(1)}, s32[1,128]{1,0:T(1,128)}, u32[]{:S(2)}) copy-start(s32[1,128]{1,0:T(1,128)} %param.25) | copy-start | bytes 1540
  134.6 264.0 %reduce-scatter.3.cloned.1.call-start = ((), (), s32[]{:S(2)}) async-start(), calls=%async_computation.5 | async-start | bytes 9437184 | tf_op jit(solution)/shard_map/reduce_scatter | solution.py:144
  170.1 21.5 %copy-start.5 = (s32[1,8192]{1,0:T(1,128)}, s32[1,8192]{1,0:T(1,128)S(1)}, u32[]{:S(2)}) copy-start(s32[1,8192]{1,0:T(1,128)S(1)} %all-gather.1) | copy-start | bytes 98308
  219.4 17.3 %copy-start.3 = (bf16[1024,128]{1,0:T(8,128)(2,1)S(1)}, bf16[1024,128]{1,0:T(8,128)(2,1)}, u32[]{:S(2)}) copy-start(bf16[1024,128]{1,0:T(8,128)(2,1)} %get-tuple-element.481) | copy-start | bytes 786436
  219.6 5.4 %copy-start.4 = (bf16[1024,128]{1,0:T(8,128)(2,1)S(1)}, bf16[1024,128]{1,0:T(8,128)(2,1)}, u32[]{:S(2)}) copy-start(bf16[1024,128]{1,0:T(8,128)(2,1)} %get-tuple-element.198) | copy-start | bytes 786436 | tf_op jit(solution)/shard_map/cond
  236.7 1.0 copy-start.2
  253.3 145.3 %copy-start.1 = (bf16[4096,128]{1,0:T(8,128)(2,1)S(1)}, bf16[4096,128]{1,0:T(8,128)(2,1)}, u32[]{:S(2)}) copy-start(bf16[4096,128]{1,0:T(8,128)(2,1)} %param.27) | copy-start | bytes 3145732
Sparse Core Ops, SparseCore 0:
  11.9 98.5 all-gather.5
  117.3 29.4 all-gather.7
  148.5 25.4 all-gather.9
  177.9 78.7 reduce-scatter.4
  262.6 136.0 reduce-scatter.2
where the time goes:
time: 411 us; the launch traced here: 405 us
  waiting for transfers between devices  233 us (57%)
  matrix products  60.3 us (15%)
  blocking collectives  34.9 us (8%)
  between operations  23.7 us (6%)
  other arithmetic  23.3 us (6%)
  local copies, waits for them, and re-layouts  16 us (4%)
  loops' own time  13.8 us (3%)
    reduce_scatter x1, waiting for transfers between devices, per_device(): lax.psum_scatter(jnp.dot(attended, w_out, preferred_element_type=jnp.floa...  134 us
    all_gather x1, waiting for transfers between devices, per_device(): shard_rows = lax.all_gather(normed, 'heads', axis=0, tiled=True)  98.7 us
    all_gather x1, blocking collectives, per_device(): seg_all = lax.all_gather(seg_ids, 'blk', axis=0, tiled=True)  20.1 us
    all_gather x1, blocking collectives, per_device(): seg_piece = lax.all_gather(segment_ids[0], 'heads', axis=0, tiled=True)  14.8 us
    dot_general x2, matrix products, attend(): jnp.einsum('kgrs,skd->kgrd', exponent.astype(jnp.bfloat16), val_part.resh...  14 us
    another operation x8, loops' own time, per_device(): lax.cond(needed, lambda state_now: attend(state_now, key_part, val_part,...  13.8 us
    dot_general x1, matrix products, per_device(): lax.dot_general(picked.reshape(row_count, span_dp * span_blk * row_share)...  9.48 us
    dot_general x1, matrix products, per_device(): jnp.dot(attended, w_out, preferred_element_type=jnp.float32)  9.08 us
  transfers between devices with their start and end apart: 5, of which 2 were waited for; matrix products, arithmetic and copies ran while one was open for 22% of the time, Pallas kernels for 0%

commit v1 on v0

v1 whole, which is shorter than its diff:
```python
import math

import jax
import jax.numpy as jnp
import numpy as np
from jax import lax
from jax.experimental import pallas as pl
from jax.experimental.pallas import tpu as pltpu
from jax.sharding import PartitionSpec as P

MESH = pl.DeviceIdType.MESH
HD = 128
D = 4096
ROWS = 128
EPSILON = 1e-05
ROPE_BASE = 500000.0
BIG = 1e30
FEATS = 16
KROWS = HD + FEATS
PAD = 4
F32 = jnp.float32
BF16 = jnp.bfloat16


def tables():
    frequency = ROPE_BASE ** (-(np.arange(64, dtype=np.float64) * 2.0 / HD))
    frequency = np.concatenate([frequency, frequency])
    base = np.arange(64)[:, None] * float(ROWS) * frequency[None, :]
    step = np.arange(ROWS)[:, None] * frequency[None, :]
    return [f(v).astype(np.float32) for v in (base, step) for f in (np.cos, np.sin)]


def dot(a, b, dims=(((1,), (0,)), ((), ()))):
    return lax.dot_general(a, b, dims, preferred_element_type=F32)


def kernel(
    tok, gain, seg, wq_h, wk_h, wv_h, wo_h, base_cos, base_sin, step_cos, step_sin,
    out, gram,
    X, WQ, WKV, WO, QE, KV, PKT, GP, GC, GX, GD, AT, AR, PT, RA, RF, ACC, TOP,
    ss, rs, kss, krs, ls,
):
    a, b, h = lax.axis_index("dp"), lax.axis_index("blk"), lax.axis_index("heads")
    x, c = b // 2, b % 2
    y, z = h // 4, h % 4
    zp, zm, zo = (z + 1) % 4, (z + 3) % 4, (z + 2) % 4
    up, down = (a, b, y * 4 + zp), (a, b, y * 4 + zm)
    side = (a, b, (1 - y) * 4 + z)
    far = (1 - a, b, (1 - y) * 4 + z)
    twin = (a, x * 2 + 1 - c, h)
    other = (1 - a, b, h)
    ring = [None] + [(a, ((x + k) % 4) * 2 + c, h) for k in (1, 2, 3)]

    loads = [
        pltpu.make_async_copy(wk_h, WKV.at[:, 0:HD], ls.at[0]),
        pltpu.make_async_copy(wv_h, WKV.at[:, HD : 2 * HD], ls.at[1]),
        pltpu.make_async_copy(wq_h, WQ, ls.at[2]),
        pltpu.make_async_copy(wo_h, WO.at[0], ls.at[3]),
    ]
    for load in loads:
        load.start()

    barrier = pltpu.get_barrier_semaphore()
    partners = [up, down, side, far, twin, other] + ring[1:]
    for partner in partners:
        pl.semaphore_signal(barrier, inc=1, device_id=partner, device_id_type=MESH)

    def normalise(i, _):
        at = pl.ds(pl.multiple_of(i * 16, 16), 16)
        values = tok[at, :].astype(F32)
        mean_square = jnp.mean(values * values, axis=-1, keepdims=True)
        X[h, at, 0:D] = (values * lax.rsqrt(mean_square + EPSILON) * gain[...]).astype(BF16)
        return 0

    lax.fori_loop(0, ROWS // 16, normalise, 0)
    feature = lax.broadcasted_iota(jnp.int32, (ROWS, ROWS), 0)
    X[h, :, D : D + ROWS] = jnp.where(feature == seg[...], 1.0, 0.0).astype(BF16)

    pl.semaphore_wait(barrier, len(partners))

    def send(i, src, dst, device):
        return pltpu.make_async_remote_copy(
            src_ref=src, dst_ref=dst, send_sem=ss.at[i], recv_sem=rs.at[i],
            device_id=device, device_id_type=MESH,
        )

    def slab(g, half=None):
        return X.at[g] if half is None else X.at[g, pl.ds(half * 64, 64)]

    hs = (1 - y) * 4 + z
    own_side = send(0, X.at[h], X.at[h], side)
    own_up = send(1, X.at[h], X.at[h], up)
    own_down = send(2, X.at[h], X.at[h], down)
    oth_up = send(3, X.at[hs], X.at[hs], up)
    oth_down = send(4, X.at[hs], X.at[hs], down)
    fw = []
    for k, col in enumerate((y, 1 - y)):
        fw.append(send(5 + 2 * k, slab(col * 4 + zm, 0), slab(col * 4 + zm, 0), up))
        fw.append(send(6 + 2 * k, slab(col * 4 + zp, 1), slab(col * 4 + zp, 1), down))
    own_side.start()
    own_up.start()
    own_down.start()
    half_rows = pl.ds(pl.multiple_of(c * 256, 256), 256)
    wo_far = send(9, wo_h.at[half_rows], WO.at[1, half_rows], far)
    wo_far.start()
    wo_twin = send(10, WO.at[1, half_rows], WO.at[1, half_rows], twin)

    pads = lax.broadcasted_iota(jnp.int32, (FEATS, HD), 0)
    for slot in range(PAD):
        KV[slot] = jnp.zeros((KROWS + HD, HD), BF16)
        KV[slot, HD:KROWS, :] = jnp.where(pads == 8, 1.0, 0.0).astype(BF16)

    def chunk_of(i):
        stage, second = i // 2, i % 2
        col = jnp.where(stage == 0, jnp.where(second == 0, y, 1 - y),
              jnp.where(stage == 1, y,
              jnp.where(stage == 2, 1 - y, jnp.where(second == 0, y, 1 - y))))
        row = jnp.where(stage == 0, z, jnp.where(stage == 3, zo, jnp.where(second == 0, zm, zp)))
        return col * 4 + row

    def kv_copy(kind, i):
        g = chunk_of(i)
        quad = [x, x, x, (x + 3) % 4, (x + 2) % 4][kind]
        device = [twin, ring[1], ring[2], twin, twin][kind]
        slot = (quad * 2 + c) * 8 + g + PAD
        return pltpu.make_async_remote_copy(
            src_ref=KV.at[slot], dst_ref=KV.at[slot], send_sem=kss.at[kind, i],
            recv_sem=krs.at[kind, i], device_id=device, device_id_type=MESH,
        )

    lane = lax.broadcasted_iota(jnp.int32, (ROWS, HD), 1)
    scale = math.log2(math.e) / math.sqrt(HD)

    def project(stage):
        ga, gb = chunk_of(2 * stage), chunk_of(2 * stage + 1)
        rows = jnp.concatenate([X[ga, :, 0:D], X[gb, :, 0:D]], axis=0)
        pair = (ga, gb)
        turns = []
        for g in pair:
            rc = b * 8 + g
            bc, bs = base_cos[pl.ds(rc, 1), :], base_sin[pl.ds(rc, 1), :]
            cosine = bc * step_cos[...] - bs * step_sin[...]
            sine = bs * step_cos[...] + bc * step_sin[...]
            turns.append((cosine, jnp.where(lane < 64, -sine, sine)))
        kv = dot(rows, WKV[...])
        for k, g in enumerate(pair):
            cosine, sine = turns[k]
            slot = b * 8 + g + PAD
            key = kv[k * ROWS : (k + 1) * ROWS, 0:HD]
            key = key * cosine + pltpu.roll(key, 64, 1) * sine
            KV[slot, 0:HD, :] = key.T.astype(BF16)
            KV[slot, HD:KROWS, :] = X[g, 0:FEATS, D : D + ROWS]
            KV[slot, KROWS : KROWS + HD, :] = kv[k * ROWS : (k + 1) * ROWS, HD : 2 * HD].astype(BF16)
        for i in (0, 1):
            for kind in range(3):
                kv_copy(kind, 2 * stage + i).start()
        for n in range(2):
            part = dot(rows, WQ[:, n * 256 : (n + 1) * 256])
            for k, g in enumerate(pair):
                cosine, sine = turns[k]
                for m in range(2):
                    head = part[k * ROWS : (k + 1) * ROWS, m * HD : (m + 1) * HD]
                    head = (head * cosine + pltpu.roll(head, 64, 1) * sine) * scale
                    at = (n * 2 + m) * ROWS
                    QE[g, at : at + ROWS, 0:HD] = head.astype(BF16)
        for g in pair:
            mine = X[g, :, D : D + ROWS].astype(F32).T
            ext = jnp.where(lane < 8, jnp.where(mine > 0.5, 0.0, -BIG), jnp.where(lane == 8, -BIG, 0.0))
            for m in range(4):
                QE[g, m * ROWS : (m + 1) * ROWS, HD : 2 * HD] = ext.astype(BF16)

    def forward_kv(stage):
        for i in (0, 1):
            for kind in (1, 2):
                kv_copy(kind, 2 * stage + i).wait_recv()
                kv_copy(kind + 2, 2 * stage + i).start()

    for load in loads[:3]:
        load.wait()

    def gather_stage(stage, _):
        @pl.when(stage == 0)
        def _():
            own_side.wait_recv()
            oth_up.start()
            oth_down.start()

        @pl.when(stage == 1)
        def _():
            own_up.wait_recv()
            fw[0].start()
            own_down.wait_recv()
            fw[1].start()

        @pl.when(stage == 2)
        def _():
            oth_up.wait_recv()
            fw[2].start()
            oth_down.wait_recv()
            fw[3].start()

        @pl.when(stage == 3)
        def _():
            for copy in fw:
                copy.wait_recv()

        project(stage)

        @pl.when(stage > 0)
        def _():
            forward_kv(stage - 1)

        return 0

    lax.fori_loop(0, 4, gather_stage, 0)

    wo_far.wait_recv()
    wo_twin.start()
    pick_row = lax.broadcasted_iota(jnp.int32, (128, 512), 0)
    pick_col = lax.broadcasted_iota(jnp.int32, (128, 512), 1)
    chosen = (pick_col == (pick_row // 32) * 128 + z * 32 + pick_row % 32)
    chosen = jnp.where(chosen, 1.0, 0.0).astype(BF16)

    for group in range(4):
        parts = []
        for n in range(4):
            q = (n % 2) * 8 + (2 * (group % 2) + n // 2) * 2 + group // 2
            at = pl.ds(pl.multiple_of(q * 256 + y * 128, 128), 128)
            parts.append(X[:, :, at].reshape(1024, 128))
        taken = jnp.concatenate(parts, axis=1)
        PKT[group * 128 : (group + 1) * 128, :] = dot(chosen, taken, (((1,), (1,)), ((), ()))).astype(BF16)

    def gram_tile(n, _):
        at = pl.ds(pl.multiple_of(n * 256, 256), 256)
        tile = dot(PKT[...], X[:, :, at].reshape(1024, 256)).astype(BF16)
        GP[0, :, at] = tile[0:256]
        GP[1, :, at] = tile[256:512]
        return 0

    lax.fori_loop(0, 16, gram_tile, 0)
    gram_twin = send(11, GP.at[1 - c], GC, twin)
    gram_twin.start()
    gram_ring = [None] + [
        send(11 + k, GP.at[c, pl.ds(pl.multiple_of(((x + k) % 4) * 64, 64), 64)], GX.at[k - 1], ring[k])
        for k in (1, 2, 3)
    ]
    gram_other = send(15, GC.at[pl.ds(pl.multiple_of((1 - a) * 32, 32), 32)], GD, other)

    forward_kv(3)

    def settle(i, _):
        kv_copy(0, i).wait_recv()
        kv_copy(3, i).wait_recv()
        kv_copy(4, i).wait_recv()
        return 0

    lax.fori_loop(0, 8, settle, 0)
    wo_twin.wait_recv()
    loads[3].wait()

    tri = lax.broadcasted_iota(jnp.int32, (512, HD), 0) % ROWS >= lax.broadcasted_iota(jnp.int32, (512, HD), 1)
    blank = jnp.zeros((256 - KROWS, HD), BF16)
    ones = jnp.ones((HD, HD), BF16)

    def attend(g):
        pc = b * 8 + g
        slot = pc + PAD
        keys = jnp.concatenate([KV[slot, 0:KROWS, :], blank], axis=0)
        scores = jnp.where(tri, dot(QE[g], keys), -BIG)
        top = jnp.max(scores, axis=1, keepdims=True)
        probs = jnp.exp2(scores - top).astype(BF16)
        ACC[...] = dot(probs, jnp.concatenate([KV[slot, KROWS : KROWS + HD, :], ones], axis=1))
        TOP[...] = jnp.broadcast_to(top, (512, HD))

        def step(t, _):
            first = slot - 4 * (t + 1)
            keys = jnp.concatenate(
                [jnp.concatenate([KV[first + j, 0:KROWS, :], blank], axis=0) for j in range(4)], axis=1)
            values = jnp.concatenate(
                [jnp.concatenate([KV[first + j, KROWS : KROWS + HD, :], ones], axis=1) for j in range(4)], axis=0)
            scores = dot(QE[g], keys)
            before = TOP[:, 0:1]
            top = jnp.maximum(before, jnp.max(scores, axis=1, keepdims=True))
            probs = jnp.exp2(scores - top).astype(BF16)
            ACC[...] = ACC[...] * jnp.exp2(before - top) + dot(probs, values)
            TOP[...] = jnp.broadcast_to(top, (512, HD))
            return 0

        lax.fori_loop(0, jnp.minimum(8, (pc + 3) // 4), step, 0)
        mixed = (ACC[:, 0:HD] / ACC[:, HD : 2 * HD]).astype(BF16)
        for m in range(4):
            AT[g, :, m * HD : (m + 1) * HD] = mixed[m * ROWS : (m + 1) * ROWS]

    turned = [
        send(16, PT.at[0, pl.ds(0, 64)], RA.at[0], up),
        send(17, PT.at[0, pl.ds(64, 64)], RA.at[1], down),
        send(18, PT.at[1], RF.at[0], up),
        send(19, PT.at[2], RF.at[1], down),
    ]

    def row_of(k):
        return jnp.where(k == 0, zo, jnp.where(k == 1, zp, jnp.where(k == 2, zm, z)))

    def swap(k):
        return pltpu.make_async_remote_copy(
            src_ref=AT.at[(1 - y) * 4 + row_of(k)], dst_ref=AR.at[k], send_sem=ss.at[20 + k],
            recv_sem=rs.at[20 + k], device_id=side, device_id_type=MESH,
        )

    def out_stage(k, _):
        row = row_of(k)

        def both(i, _):
            attend(jnp.where(i == 0, 1 - y, y) * 4 + row)

            @pl.when(i == 0)
            def _():
                swap(k).start()

            return 0

        lax.fori_loop(0, 2, both, 0)
        swap(k).wait_recv()

        def out_tile(n, _):
            at = pl.ds(pl.multiple_of(n * 512, 512), 512)
            PT[k, :, at] = (dot(AT[y * 4 + row], WO[0, :, at]) + dot(AR[k], WO[1, :, at])).astype(BF16)
            return 0

        lax.fori_loop(0, 8, out_tile, 0)

        @pl.when(k == 0)
        def _():
            turned[0].start()
            turned[1].start()
            gram_twin.wait_recv()

            def add(n, _):
                at = pl.ds(pl.multiple_of(n * 512, 512), 512)
                GP[c, :, at] = (GP[c, :, at].astype(F32) + GC[:, at].astype(F32)).astype(BF16)
                return 0

            lax.fori_loop(0, 8, add, 0)
            for k in (1, 2, 3):
                gram_ring[k].start()

        for which in (0, 1):
            @pl.when(k == 1 + which)
            def _(which=which):
                turned[which].wait_recv()
                at = pl.ds(64 * which, 64)
                PT[1 + which, at] = (PT[1 + which, at].astype(F32) + RA[which].astype(F32)).astype(BF16)
                turned[2 + which].start()

        @pl.when(k == 2)
        def _():
            for k in (1, 2, 3):
                gram_ring[k].wait_recv()

            def add(n, _):
                at = pl.ds(pl.multiple_of(n * 512, 512), 512)
                total = GP[c, pl.ds(pl.multiple_of(x * 64, 64), 64), at].astype(F32)
                for k in range(3):
                    total = total + GX[k, :, at].astype(F32)
                GC[0:64, at] = total.astype(BF16)
                return 0

            lax.fori_loop(0, 8, add, 0)
            gram_other.start()

        return 0

    lax.fori_loop(0, 4, out_stage, 0)
    gram_other.wait_recv()
    mine = pl.ds(pl.multiple_of(a * 32, 32), 32)
    gram[...] = (GC[mine, :].astype(F32) + GD[...].astype(F32)) * (1.0 / 16384.0)
    turned[2].wait_recv()
    turned[3].wait_recv()
    out[...] = (PT[3].astype(F32) + RF[0].astype(F32) + RF[1].astype(F32)).astype(BF16)

    for copy in [own_side, own_up, own_down, oth_up, oth_down, *fw, wo_far, wo_twin, gram_twin,
                 *gram_ring[1:], gram_other, *turned]:
        copy.wait_send()

    def drain(i, _):
        for kind in range(5):
            kv_copy(kind, i).wait_send()
        return 0

    lax.fori_loop(0, 8, drain, 0)

    def drain_swap(k, _):
        swap(k).wait_send()
        return 0

    lax.fori_loop(0, 4, drain_swap, 0)


def per_device(tokens, norm_gain, segment_ids, w_query, w_key, w_value, w_out):
    vmem = pl.BlockSpec(memory_space=pltpu.VMEM)
    hbm = pl.BlockSpec(memory_space=pl.ANY)
    dma = pltpu.SemaphoreType.DMA
    scratch = [
        pltpu.VMEM((8, ROWS, D + ROWS), BF16),
        pltpu.VMEM((D, 512), BF16),
        pltpu.VMEM((D, 256), BF16),
        pltpu.VMEM((2, 512, D), BF16),
        pltpu.VMEM((8, 512, 256), BF16),
        pltpu.VMEM((64 + PAD, KROWS + HD, HD), BF16),
        pltpu.VMEM((512, 1024), BF16),
        pltpu.VMEM((2, 256, D), BF16),
        pltpu.VMEM((256, D), BF16),
        pltpu.VMEM((3, 64, D), BF16),
        pltpu.VMEM((32, D), BF16),
        pltpu.VMEM((8, ROWS, 512), BF16),
        pltpu.VMEM((4, ROWS, 512), BF16),
        pltpu.VMEM((4, ROWS, D), BF16),
        pltpu.VMEM((2, 64, D), BF16),
        pltpu.VMEM((2, ROWS, D), BF16),
        pltpu.VMEM((512, 256), F32),
        pltpu.VMEM((512, HD), F32),
        dma((24,)),
        dma((24,)),
        dma((5, 8)),
        dma((5, 8)),
        dma((4,)),
    ]
    delta, gram = pl.pallas_call(
        kernel,
        out_shape=(jax.ShapeDtypeStruct((ROWS, D), BF16), jax.ShapeDtypeStruct((32, D), F32)),
        in_specs=[vmem, vmem, vmem, hbm, hbm, hbm, hbm, vmem, vmem, vmem, vmem],
        out_specs=(vmem, vmem),
        scratch_shapes=scratch,
        compiler_params=pltpu.CompilerParams(
            collective_id=0, has_side_effects=True, vmem_limit_bytes=62 << 20),
        name="sublayer",
    )(tokens[0], norm_gain[None], segment_ids, w_query, w_key, w_value, w_out,
      *[jnp.asarray(t) for t in tables()])
    return delta[None], gram


def solution(mesh):
    return jax.shard_map(
        per_device,
        mesh=mesh,
        in_specs=(
            P("dp", ("blk", "heads"), None),
            P(),
            P("dp", ("blk", "heads")),
            P(None, "heads"),
            P(None, "heads"),
            P(None, "heads"),
            P("heads", None),
        ),
        out_specs=(P("dp", ("blk", "heads"), None), P(("dp", "blk", "heads"), None)),
        check_vma=False,
    )
```

time: 411 us -> 182 us (0.44)
  the two profiles are of different devices: /device:TPU:1 before, /device:TPU:5 now
where the time goes in v1:
time: 182 us
  Pallas kernels  177 us (97%)
  local copies, waits for them, and re-layouts  4.16 us (2%)
    pallas_call x1, Pallas kernels, per_device(): pl.pallas_call(kernel, out_shape=(jax.ShapeDtypeStruct((ROWS, D), BF16),...  177 us
    unnamed x2, local copies, waits for them, and re-layouts  4.16 us

profile of v1, /device:TPU:5, one launch (start us, length us, event | category | flops | bytes accessed | tf_op | source)
XLA Modules:
  0.0 182.1 jit_solution(15382688201418352492)
XLA Ops:
  0.6 177.3 %sublayer.1 = (bf16[128,4096]{1,0:T(8,128)(2,1)}, f32[32,4096]{1,0:T(8,128)}) custom-call(bf16[128,4096]{1,0:T(8,128)(2,1)} %bitcast.3, f32[1,4096]{1,0:T(1,128)} %bitcast.5, s32[1,128]{1,0:T(1,128)} %seg.1, bf16[4096,512]{1,0:T(8,128)(2,1)} %wq_h.1, bf16[4096,128]{1,0:T(8,128)(2,1)} %wk_h.1, bf16[4096,128]{1,0:T(8,128)(2,1)} %wv_h.1, ...), custom_call_target="tpu_custom_call" | custom-call | tf_op jit(solution)/shard_map/sublayer/pallas_call | solution.py:428
  177.9 2.3 %copy.15 = bf16[1,128,4096]{2,1,0:T(8,128)(2,1)} copy(bf16[1,128,4096]{2,1,0:T(8,128)(2,1)} %bitcast.4) | data formatting | bytes 2097152
  180.2 1.9 %copy.16 = f32[32,4096]{1,0:T(8,128)} copy(f32[32,4096]{1,0:T(8,128)} %get-tuple-element.9) | data formatting | bytes 1048576

commit v2 on v1

v2 whole, which is shorter than its diff:
```python
import math

import jax
import jax.numpy as jnp
import numpy as np
from jax import lax
from jax.experimental import pallas as pl
from jax.experimental.pallas import tpu as pltpu
from jax.sharding import PartitionSpec as P

MESH = pl.DeviceIdType.MESH
HD = 128
D = 4096
ROWS = 128
EPSILON = 1e-05
ROPE_BASE = 500000.0
BIG = 1e30
FEATS = 16
KROWS = HD + FEATS
PAD = 8
CUT = 18 * 128
WINDOW = 4096
F32 = jnp.float32
BF16 = jnp.bfloat16


def tables():
    frequency = ROPE_BASE ** (-(np.arange(64, dtype=np.float64) * 2.0 / HD))
    frequency = np.concatenate([frequency, frequency])
    base = np.arange(64)[:, None] * float(ROWS) * frequency[None, :]
    step = np.arange(ROWS)[:, None] * frequency[None, :]
    return [f(v).astype(np.float32) for v in (base, step) for f in (np.cos, np.sin)]


def dot(a, b, dims=(((1,), (0,)), ((), ()))):
    return lax.dot_general(a, b, dims, preferred_element_type=F32)


def kernel(
    tok, gain, seg, wq_h, wk_h, wv_h, wo_h, base_cos, base_sin, step_cos, step_sin,
    out, gram,
    X, WQ, WKV, WO, QE, KV, PKT, GP, GC, GX, GD, AT, AR, PT, RA, RF, ACC, TOP, S0, S1, M0, M1,
    ss, rs, kss, krs, sws, swr, ls,
):
    a, b, h = lax.axis_index("dp"), lax.axis_index("blk"), lax.axis_index("heads")
    x, c = b // 2, b % 2
    y, z = h // 4, h % 4
    zp, zm, zo = (z + 1) % 4, (z + 3) % 4, (z + 2) % 4
    up, down = (a, b, y * 4 + zp), (a, b, y * 4 + zm)
    side = (a, b, (1 - y) * 4 + z)
    far = (1 - a, b, (1 - y) * 4 + z)
    twin = (a, x * 2 + 1 - c, h)
    other = (1 - a, b, h)
    ring = [None] + [(a, ((x + k) % 4) * 2 + c, h) for k in (1, 2, 3)]

    loads = [
        pltpu.make_async_copy(wk_h, WKV.at[:, 0:HD], ls.at[0]),
        pltpu.make_async_copy(wv_h, WKV.at[:, HD : 2 * HD], ls.at[1]),
        pltpu.make_async_copy(wq_h, WQ, ls.at[2]),
        pltpu.make_async_copy(wo_h, WO.at[0], ls.at[3]),
    ]
    for load in loads:
        load.start()

    barrier = pltpu.get_barrier_semaphore()
    partners = [up, down, side, far, twin, other] + ring[1:]
    for partner in partners:
        pl.semaphore_signal(barrier, inc=1, device_id=partner, device_id_type=MESH)

    def normalise(i, _):
        at = pl.ds(pl.multiple_of(i * 16, 16), 16)
        values = tok[at, :].astype(F32)
        mean_square = jnp.mean(values * values, axis=-1, keepdims=True)
        X[h, at, 0:D] = (values * lax.rsqrt(mean_square + EPSILON) * gain[...]).astype(BF16)
        return 0

    lax.fori_loop(0, ROWS // 16, normalise, 0)
    feature = lax.broadcasted_iota(jnp.int32, (ROWS, ROWS), 0)
    X[h, :, D : D + ROWS] = jnp.where(feature == seg[...], 1.0, 0.0).astype(BF16)

    pl.semaphore_wait(barrier, len(partners))

    def send(i, src, dst, device):
        return pltpu.make_async_remote_copy(
            src_ref=src, dst_ref=dst, send_sem=ss.at[i], recv_sem=rs.at[i],
            device_id=device, device_id_type=MESH,
        )

    FIRST, LAST = pl.ds(0, CUT), pl.ds(CUT, D + ROWS - CUT)

    def move(i, g, columns, device, half=None):
        rows = pl.ds(0, ROWS) if half is None else pl.ds(half * 64, 64)
        return send(i, X.at[g, rows, columns], X.at[g, rows, columns], device)

    hs = (1 - y) * 4 + z
    om, op, oo = y * 4 + zm, y * 4 + zp, y * 4 + zo
    nm, np_ = (1 - y) * 4 + zm, (1 - y) * 4 + zp
    y_first = move(0, h, FIRST, side)
    y_last = move(1, h, LAST, side)
    z_first = [move(2, h, FIRST, up), move(3, h, FIRST, down)]
    z_last = [move(4, h, LAST, up), move(5, h, LAST, down)]
    n_first = [move(6, hs, FIRST, up), move(7, hs, FIRST, down)]
    half_first = [move(8, om, FIRST, up, 0), move(9, op, FIRST, down, 1)]
    half_last = [move(10, om, LAST, up, 0), move(11, op, LAST, down, 1)]
    y_near = [move(12, om, LAST, side), move(13, op, LAST, side)]
    y_oppo = [move(14, oo, LAST, side, 0), move(15, oo, LAST, side, 1)]
    half_next = [move(16, nm, FIRST, up, 0), move(17, np_, FIRST, down, 1)]
    gathers = [y_first, y_last, *z_first, *z_last, *n_first, *half_first, *half_last, *y_near, *y_oppo, *half_next]
    for copy in (y_first, *z_last, *z_first, y_last):
        copy.start()
    half_rows = pl.ds(pl.multiple_of(c * 256, 256), 256)
    wo_far = send(18, wo_h.at[half_rows], WO.at[1, half_rows], far)
    wo_far.start()
    wo_twin = send(19, WO.at[1, half_rows], WO.at[1, half_rows], twin)

    pads = lax.broadcasted_iota(jnp.int32, (FEATS, HD), 0)
    def clear(slot, _):
        KV[slot] = jnp.zeros((KROWS + HD, HD), BF16)
        KV[slot, HD:KROWS, :] = jnp.where(pads == 8, 1.0, 0.0).astype(BF16)
        return 0

    lax.fori_loop(0, PAD, clear, 0)

    def chunk_of(i):
        stage, second = i // 2, i % 2
        col = jnp.where(stage == 0, jnp.where(second == 0, y, 1 - y),
              jnp.where(stage == 1, y,
              jnp.where(stage == 2, 1 - y, jnp.where(second == 0, y, 1 - y))))
        row = jnp.where(stage == 0, z, jnp.where(stage == 3, zo, jnp.where(second == 0, zm, zp)))
        return col * 4 + row

    def kv_copy(kind, i):
        g = chunk_of(i)
        quad = [x, x, x, (x + 3) % 4, (x + 2) % 4][kind]
        device = [twin, ring[1], ring[2], twin, twin][kind]
        slot = (quad * 2 + c) * 8 + g + PAD
        return pltpu.make_async_remote_copy(
            src_ref=KV.at[slot], dst_ref=KV.at[slot], send_sem=kss.at[kind, i],
            recv_sem=krs.at[kind, i], device_id=device, device_id_type=MESH,
        )

    lane = lax.broadcasted_iota(jnp.int32, (ROWS, HD), 1)
    scale = math.log2(math.e) / math.sqrt(HD)

    def project(stage):
        ga, gb = chunk_of(2 * stage), chunk_of(2 * stage + 1)
        rows = jnp.concatenate([X[ga, :, 0:D], X[gb, :, 0:D]], axis=0)
        pair = (ga, gb)
        turns = []
        for g in pair:
            rc = b * 8 + g
            bc, bs = base_cos[pl.ds(rc, 1), :], base_sin[pl.ds(rc, 1), :]
            cosine = bc * step_cos[...] - bs * step_sin[...]
            sine = bs * step_cos[...] + bc * step_sin[...]
            turns.append((cosine, jnp.where(lane < 64, -sine, sine)))
        kv = dot(rows, WKV[...])
        for k, g in enumerate(pair):
            cosine, sine = turns[k]
            slot = b * 8 + g + PAD
            key = kv[k * ROWS : (k + 1) * ROWS, 0:HD]
            key = key * cosine + pltpu.roll(key, 64, 1) * sine
            KV[slot, 0:HD, :] = key.T.astype(BF16)
            KV[slot, HD:KROWS, :] = X[g, 0:FEATS, D : D + ROWS]
            KV[slot, KROWS : KROWS + HD, :] = kv[k * ROWS : (k + 1) * ROWS, HD : 2 * HD].astype(BF16)
        for i in (0, 1):
            for kind in range(3):
                kv_copy(kind, 2 * stage + i).start()
        for n in range(2):
            part = dot(rows, WQ[:, n * 256 : (n + 1) * 256])
            for k, g in enumerate(pair):
                cosine, sine = turns[k]
                for m in range(2):
                    head = part[k * ROWS : (k + 1) * ROWS, m * HD : (m + 1) * HD]
                    head = (head * cosine + pltpu.roll(head, 64, 1) * sine) * scale
                    for half in range(2):
                        at = half * 256 + (n * 2 + m) * 64
                        QE[g, at : at + 64, 0:HD] = head[half * 64 : half * 64 + 64].astype(BF16)
        for g in pair:
            mine = X[g, :, D : D + ROWS].astype(F32).T
            ext = jnp.where(lane < 8, jnp.where(mine > 0.5, 0.0, -BIG), jnp.where(lane == 8, -BIG, 0.0))
            for m in range(8):
                at = (m // 4) * 64
                QE[g, m * 64 : m * 64 + 64, HD : 2 * HD] = ext[at : at + 64].astype(BF16)

    def forward_kv(stage):
        for i in (0, 1):
            for kind in (1, 2):
                kv_copy(kind, 2 * stage + i).wait_recv()
                kv_copy(kind + 2, 2 * stage + i).start()

    for load in loads[:3]:
        load.wait()

    pick_row = lax.broadcasted_iota(jnp.int32, (128, 512), 0)
    pick_col = lax.broadcasted_iota(jnp.int32, (128, 512), 1)
    chosen = (pick_col == (pick_row // 32) * 128 + z * 32 + pick_row % 32)
    chosen = jnp.where(chosen, 1.0, 0.0).astype(BF16)

    def gram_rows(last):
        slabs = [chunk_of(i) for i in ((6, 7) if last else range(6))]
        count = len(slabs) * ROWS
        for group in range(4):
            parts = []
            for n in range(4):
                q = (n % 2) * 8 + (2 * (group % 2) + n // 2) * 2 + group // 2
                at = pl.ds(pl.multiple_of(q * 256 + y * 128, 128), 128)
                parts.append(jnp.concatenate([X[g, :, at] for g in slabs], axis=0))
            taken = jnp.concatenate(parts, axis=1)
            picked = dot(chosen, taken, (((1,), (1,)), ((), ())))
            PKT[group * 128 : (group + 1) * 128, 0:count] = picked.astype(BF16)

        def gram_tile(n, _):
            at = pl.ds(pl.multiple_of(n * 256, 256), 256)
            tile = dot(PKT[:, 0:count], jnp.concatenate([X[g, :, at] for g in slabs], axis=0))
            if last:
                GP[0, :, at] = (tile[0:256] + S0[:, at]).astype(BF16)
                GP[1, :, at] = (tile[256:512] + S1[:, at]).astype(BF16)
            else:
                S0[:, at] = tile[0:256]
                S1[:, at] = tile[256:512]
            return 0

        lax.fori_loop(0, 16, gram_tile, 0)

    def gather_stage(stage, _):
        @pl.when(stage == 0)
        def _():
            for k in (0, 1):
                z_last[k].wait_recv()
                half_last[k].start()
                y_near[k].start()
            y_first.wait_recv()
            for k in (0, 1):
                n_first[k].start()
            for k in (0, 1):
                z_first[k].wait_recv()
                half_first[k].start()
            y_last.wait_recv()

        @pl.when(stage == 1)
        def _():
            for k in (0, 1):
                half_last[k].wait_recv()
                y_oppo[k].start()

        @pl.when(stage == 2)
        def _():
            for k in (0, 1):
                n_first[k].wait_recv()
                half_next[k].start()
            for copy in y_near:
                copy.wait_recv()

        @pl.when(stage == 3)
        def _():
            gram_rows(False)
            for copy in (*half_first, *half_next, *y_oppo):
                copy.wait_recv()

        project(stage)

        @pl.when(stage > 0)
        def _():
            forward_kv(stage - 1)

        return 0

    lax.fori_loop(0, 4, gather_stage, 0)

    wo_far.wait_recv()
    wo_twin.start()
    gram_rows(True)
    gram_twin = send(20, GP.at[1 - c], GC, twin)
    gram_twin.start()
    gram_ring = [None] + [
        send(20 + k, GP.at[c, pl.ds(pl.multiple_of(((x + k) % 4) * 64, 64), 64)], GX.at[k - 1], ring[k])
        for k in (1, 2, 3)
    ]
    gram_other = send(24, GC.at[pl.ds(pl.multiple_of((1 - a) * 32, 32), 32)], GD, other)

    forward_kv(3)

    def settle(i, _):
        kv_copy(0, i).wait_recv()
        kv_copy(3, i).wait_recv()
        kv_copy(4, i).wait_recv()
        return 0

    lax.fori_loop(0, 8, settle, 0)
    wo_twin.wait_recv()
    loads[3].wait()

    late = lax.broadcasted_iota(jnp.int32, (256, HD), 0) % 64 - lax.broadcasted_iota(jnp.int32, (256, HD), 1)
    blank = jnp.zeros((256 - KROWS, HD), BF16)
    ones = jnp.ones((HD, HD), BF16)
    steps = jnp.minimum(4, b + 1)

    def rows_of(half):
        return pl.ds(pl.multiple_of(half * 256, 256), 256)

    def keys_of(slot):
        return jnp.concatenate([KV[slot, 0:KROWS, :], blank], axis=0)

    def values_of(slot):
        return jnp.concatenate([KV[slot, KROWS : KROWS + HD, :], ones], axis=1)

    def score_first(g, half, S, MX):
        scores = jnp.where(late + half * 64 >= 0, dot(QE[g, rows_of(half), :], keys_of(b * 8 + g + PAD)), -BIG)
        S[:, WINDOW : WINDOW + HD] = scores
        MX[...] = scores

    def score_step(g, half, S, MX, t):
        first = b * 8 + g + PAD - 8 * (t + 1)
        keys = jnp.concatenate([keys_of(first + j) for j in range(8)], axis=1)
        scores = dot(QE[g, rows_of(half), :], keys)
        S[:, pl.ds(pl.multiple_of(t * 1024, 1024), 1024)] = scores
        top = MX[...]
        for j in range(8):
            top = jnp.maximum(top, scores[:, j * HD : (j + 1) * HD])
        MX[...] = top

    def mix_first(g, S, MX):
        top = jnp.max(MX[...], axis=1, keepdims=True)
        TOP[...] = jnp.broadcast_to(top, (256, HD))
        probs = jnp.exp2(S[:, WINDOW : WINDOW + HD] - TOP[...]).astype(BF16)
        ACC[...] = dot(probs, values_of(b * 8 + g + PAD))

    def mix_step(g, S, t):
        first = b * 8 + g + PAD - 8 * (t + 1)
        values = jnp.concatenate([values_of(first + j) for j in range(8)], axis=0)
        scores = S[:, pl.ds(pl.multiple_of(t * 1024, 1024), 1024)]
        top = TOP[...]
        probs = jnp.concatenate(
            [jnp.exp2(scores[:, j * HD : (j + 1) * HD] - top).astype(BF16) for j in range(8)], axis=1)
        ACC[...] += dot(probs, values)

    def mix_last(g, half):
        mixed = (ACC[:, 0:HD] / ACC[:, HD : 2 * HD]).astype(BF16)
        rows = pl.ds(pl.multiple_of(half * 64, 64), 64)
        for m in range(4):
            AT[g, rows, m * HD : (m + 1) * HD] = mixed[m * 64 : m * 64 + 64]

    def both(g, half, S, MX, next_g, next_half, next_S, next_MX):
        mix_first(g, S, MX)
        score_first(next_g, next_half, next_S, next_MX)

        def step(t, _):
            score_step(next_g, next_half, next_S, next_MX, t)
            mix_step(g, S, t)
            return 0

        lax.fori_loop(0, steps, step, 0)
        mix_last(g, half)

    top, low = pl.ds(0, 64), pl.ds(64, 64)
    turned = [
        send(25, PT.at[0, top], RA.at[0], up),
        send(26, PT.at[0, low], RA.at[1], down),
        send(27, PT.at[1, top], RF.at[0, low], up),
        send(28, PT.at[1, low], RF.at[1, top], down),
        send(29, PT.at[2, top], RF.at[0, top], up),
        send(30, PT.at[2, low], RF.at[1, low], down),
    ]

    def part_of(k, second):
        row = jnp.where(k == 0, zo, jnp.where(k == 3, z, jnp.where(second == 0, zp, zm)))
        half = jnp.where(k == 1, 1 - second, second)
        return row, half

    def swap(k, second):
        row, half = part_of(k, second)
        rows = pl.ds(pl.multiple_of(half * 64, 64), 64)
        to = pl.ds(pl.multiple_of(second * 64, 64), 64)
        return pltpu.make_async_remote_copy(
            src_ref=AT.at[(1 - y) * 4 + row, rows], dst_ref=AR.at[k, to], send_sem=sws.at[k, second],
            recv_sem=swr.at[k, second], device_id=side, device_id_type=MESH,
        )

    def out_stage(k, _):
        rows = [part_of(k, 0), part_of(k, 1)]

        def unit(i, _):
            col = jnp.where(i == 0, 1 - y, y) * 4
            after = jnp.minimum(2 * k + i + 1, 7)
            after_col = jnp.where(after % 2 == 0, 1 - y, y) * 4
            after_row, after_half = part_of(after // 2, 0)
            both(col + rows[0][0], rows[0][1], S0, M0, col + rows[1][0], rows[1][1], S1, M1)

            @pl.when(i == 0)
            def _():
                swap(k, 0).start()

            both(col + rows[1][0], rows[1][1], S1, M1, after_col + after_row, after_half, S0, M0)

            @pl.when(i == 0)
            def _():
                swap(k, 1).start()

            return 0

        lax.fori_loop(0, 2, unit, 0)
        swap(k, 0).wait_recv()
        swap(k, 1).wait_recv()
        own = jnp.concatenate(
            [AT[y * 4 + row, pl.ds(pl.multiple_of(half * 64, 64), 64), :] for row, half in rows], axis=0)

        def out_tile(n, _):
            at = pl.ds(pl.multiple_of(n * 512, 512), 512)
            PT[k, :, at] = (dot(own, WO[0, :, at]) + dot(AR[k], WO[1, :, at])).astype(BF16)
            return 0

        lax.fori_loop(0, 8, out_tile, 0)

        @pl.when(k == 0)
        def _():
            turned[0].start()
            turned[1].start()
            gram_twin.wait_recv()

            def add(n, _):
                at = pl.ds(pl.multiple_of(n * 512, 512), 512)
                GP[c, :, at] = (GP[c, :, at].astype(F32) + GC[:, at].astype(F32)).astype(BF16)
                return 0

            lax.fori_loop(0, 8, add, 0)
            for k in (1, 2, 3):
                gram_ring[k].start()

        @pl.when(k == 1)
        def _():
            turned[2].start()
            turned[3].start()

        @pl.when(k == 2)
        def _():
            for which in (0, 1):
                turned[which].wait_recv()
                at = pl.ds(64 * which, 64)
                PT[2, at] = (PT[2, at].astype(F32) + RA[which].astype(F32)).astype(BF16)
                turned[4 + which].start()

        @pl.when(k == 2)
        def _():
            for k in (1, 2, 3):
                gram_ring[k].wait_recv()

            def add(n, _):
                at = pl.ds(pl.multiple_of(n * 512, 512), 512)
                total = GP[c, pl.ds(pl.multiple_of(x * 64, 64), 64), at].astype(F32)
                for k in range(3):
                    total = total + GX[k, :, at].astype(F32)
                GC[0:64, at] = total.astype(BF16)
                return 0

            lax.fori_loop(0, 8, add, 0)
            gram_other.start()

        return 0

    start_g = (1 - y) * 4 + zo
    score_first(start_g, 0, S0, M0)

    def start_step(t, _):
        score_step(start_g, 0, S0, M0, t)
        return 0

    lax.fori_loop(0, steps, start_step, 0)
    lax.fori_loop(0, 4, out_stage, 0)
    gram_other.wait_recv()
    mine = pl.ds(pl.multiple_of(a * 32, 32), 32)
    gram[...] = GC[mine, :].astype(F32) + GD[...].astype(F32)
    for copy in turned[2:]:
        copy.wait_recv()
    out[...] = PT[3].astype(F32) + RF[0].astype(F32) + RF[1].astype(F32)

    for copy in [*gathers, wo_far, wo_twin, gram_twin,
                 *gram_ring[1:], gram_other, *turned]:
        copy.wait_send()

    def drain(i, _):
        for kind in range(5):
            kv_copy(kind, i).wait_send()
        return 0

    lax.fori_loop(0, 8, drain, 0)

    def drain_swap(k, _):
        swap(k, 0).wait_send()
        swap(k, 1).wait_send()
        return 0

    lax.fori_loop(0, 4, drain_swap, 0)


def per_device(tokens, norm_gain, segment_ids, w_query, w_key, w_value, w_out):
    vmem = pl.BlockSpec(memory_space=pltpu.VMEM)
    hbm = pl.BlockSpec(memory_space=pl.ANY)
    dma = pltpu.SemaphoreType.DMA
    scratch = [
        pltpu.VMEM((8, ROWS, D + ROWS), BF16),
        pltpu.VMEM((D, 512), BF16),
        pltpu.VMEM((D, 256), BF16),
        pltpu.VMEM((2, 512, D), BF16),
        pltpu.VMEM((8, 512, 256), BF16),
        pltpu.VMEM((64 + PAD, KROWS + HD, HD), BF16),
        pltpu.VMEM((512, 768), BF16),
        pltpu.VMEM((2, 256, D), BF16),
        pltpu.VMEM((256, D), BF16),
        pltpu.VMEM((3, 64, D), BF16),
        pltpu.VMEM((32, D), BF16),
        pltpu.VMEM((8, ROWS, 512), BF16),
        pltpu.VMEM((4, ROWS, 512), BF16),
        pltpu.VMEM((4, ROWS, D), BF16),
        pltpu.VMEM((2, 64, D), BF16),
        pltpu.VMEM((2, ROWS, D), BF16),
        pltpu.VMEM((256, 256), F32),
        pltpu.VMEM((256, HD), F32),
        pltpu.VMEM((256, WINDOW + HD), F32),
        pltpu.VMEM((256, WINDOW + HD), F32),
        pltpu.VMEM((256, HD), F32),
        pltpu.VMEM((256, HD), F32),
        dma((40,)),
        dma((40,)),
        dma((5, 8)),
        dma((5, 8)),
        dma((4, 2)),
        dma((4, 2)),
        dma((4,)),
    ]
    delta, gram = pl.pallas_call(
        kernel,
        out_shape=(jax.ShapeDtypeStruct((ROWS, D), F32), jax.ShapeDtypeStruct((32, D), F32)),
        in_specs=[vmem, vmem, vmem, hbm, hbm, hbm, hbm, vmem, vmem, vmem, vmem],
        out_specs=(vmem, vmem),
        scratch_shapes=scratch,
        compiler_params=pltpu.CompilerParams(
            collective_id=0, has_side_effects=True, vmem_limit_bytes=62 << 20),
        name="sublayer",
    )(tokens[0], norm_gain[None], segment_ids, w_query, w_key, w_value, w_out,
      *[jnp.asarray(t) for t in tables()])
    return delta.astype(BF16)[None], gram * (1.0 / 16384.0)


def solution(mesh):
    return jax.shard_map(
        per_device,
        mesh=mesh,
        in_specs=(
            P("dp", ("blk", "heads"), None),
            P(),
            P("dp", ("blk", "heads")),
            P(None, "heads"),
            P(None, "heads"),
            P(None, "heads"),
            P("heads", None),
        ),
        out_specs=(P("dp", ("blk", "heads"), None), P(("dp", "blk", "heads"), None)),
        check_vma=False,
    )
```

time: 182 us -> 135 us (0.74)
  the two profiles are of different devices: /device:TPU:5 before, /device:TPU:1 now
where the time goes in v2:
time: 135 us
  Pallas kernels  129 us (96%)
  other arithmetic  4.56 us (3%)
    pallas_call x1, Pallas kernels, per_device(): pl.pallas_call(kernel, out_shape=(jax.ShapeDtypeStruct((ROWS, D), F32), j...  129 us

profile of v2, /device:TPU:1, one launch (start us, length us, event | category | flops | bytes accessed | tf_op | source)
XLA Modules:
  0.0 134.6 jit_solution(14479129815413060104)
XLA Ops:
  0.6 129.4 %sublayer.1 = (f32[128,4096]{1,0:T(8,128)}, f32[32,4096]{1,0:T(8,128)}) custom-call(bf16[128,4096]{1,0:T(8,128)(2,1)} %bitcast.4, f32[1,4096]{1,0:T(1,128)} %bitcast.5, s32[1,128]{1,0:T(1,128)} %seg.1, bf16[4096,512]{1,0:T(8,128)(2,1)} %wq_h.1, bf16[4096,128]{1,0:T(8,128)(2,1)} %wk_h.1, bf16[4096,128]{1,0:T(8,128)(2,1)} %wv_h.1, bf16[512,4096]{1,0:T(8,128)(2,1)} %wo_h.1, ...), custom_call_target="tpu_custom_call" | custom-call | tf_op jit(solution)/shard_map/sublayer/pallas_call | solution.py:530
  130.1 2.7 %convert_bitcast_fusion = bf16[1,128,4096]{2,1,0:T(8,128)(2,1)} fusion(f32[128,4096]{1,0:T(8,128)} %get-tuple-element.4), kind=kLoop, calls=%fused_computation | loop fusion | flops 524288 | bytes 3145728 | tf_op jit(solution)/shard_map/broadcast_in_dim | solution.py:541
  132.8 1.9 %broadcast_multiply_fusion = f32[32,4096]{1,0:T(8,128)} fusion(f32[32,4096]{1,0:T(8,128)} %get-tuple-element.5), kind=kLoop, calls=%fused_computation.1 | loop fusion | flops 131072 | bytes 1048576 | tf_op jit(solution)/shard_map/mul | solution.py:541

commit v3 on v2

--- a/solution.py
+++ b/solution.py
@@ -17,7 +17,10 @@
 BIG = 1e30
 FEATS = 16
 KROWS = HD + FEATS
-PAD = 8
+SPAN = 16
+OUT = 4096
+TILE = 1024
+PAD = SPAN
 CUT = 18 * 128
 WINDOW = 4096
 F32 = jnp.float32
@@ -39,8 +42,8 @@
 def kernel(
     tok, gain, seg, wq_h, wk_h, wv_h, wo_h, base_cos, base_sin, step_cos, step_sin,
     out, gram,
-    X, WQ, WKV, WO, QE, KV, PKT, GP, GC, GX, GD, AT, AR, PT, RA, RF, ACC, TOP, S0, S1, M0, M1,
-    ss, rs, kss, krs, sws, swr, ls,
+    X, WQ, WKV, WO, QE, KV, PKT, GP, GC, GX, GT, GD, AT, AR, PT, RA, RF, ACC, TOP, S0, S1, M0, M1,
+    ss, rs, kss, krs, sws, swr, gss, grs, ls,
 ):
     a, b, h = lax.axis_index("dp"), lax.axis_index("blk"), lax.axis_index("heads")
     x, c = b // 2, b % 2
@@ -142,10 +145,9 @@
     lane = lax.broadcasted_iota(jnp.int32, (ROWS, HD), 1)
     scale = math.log2(math.e) / math.sqrt(HD)
 
-    def project(stage):
-        ga, gb = chunk_of(2 * stage), chunk_of(2 * stage + 1)
-        rows = jnp.concatenate([X[ga, :, 0:D], X[gb, :, 0:D]], axis=0)
-        pair = (ga, gb)
+    def project(items):
+        pair = [chunk_of(i) for i in items]
+        rows = jnp.concatenate([X[g, :, 0:D] for g in pair], axis=0)
         turns = []
         for g in pair:
             rc = b * 8 + g
@@ -162,9 +164,9 @@
             KV[slot, 0:HD, :] = key.T.astype(BF16)
             KV[slot, HD:KROWS, :] = X[g, 0:FEATS, D : D + ROWS]
             KV[slot, KROWS : KROWS + HD, :] = kv[k * ROWS : (k + 1) * ROWS, HD : 2 * HD].astype(BF16)
-        for i in (0, 1):
+        for i in items:
             for kind in range(3):
-                kv_copy(kind, 2 * stage + i).start()
+                kv_copy(kind, i).start()
         for n in range(2):
             part = dot(rows, WQ[:, n * 256 : (n + 1) * 256])
             for k, g in enumerate(pair):
@@ -182,11 +184,11 @@
                 at = (m // 4) * 64
                 QE[g, m * 64 : m * 64 + 64, HD : 2 * HD] = ext[at : at + 64].astype(BF16)
 
-    def forward_kv(stage):
-        for i in (0, 1):
+    def forward_kv(items):
+        for i in items:
             for kind in (1, 2):
-                kv_copy(kind, 2 * stage + i).wait_recv()
-                kv_copy(kind + 2, 2 * stage + i).start()
+                kv_copy(kind, i).wait_recv()
+                kv_copy(kind + 2, i).start()
 
     for load in loads[:3]:
         load.wait()
@@ -195,6 +197,26 @@
     pick_col = lax.broadcasted_iota(jnp.int32, (128, 512), 1)
     chosen = (pick_col == (pick_row // 32) * 128 + z * 32 + pick_row % 32)
     chosen = jnp.where(chosen, 1.0, 0.0).astype(BF16)
+
+    def tile_copy(kind, n, src, dst, device):
+        return pltpu.make_async_remote_copy(
+            src_ref=src, dst_ref=dst, send_sem=gss.at[kind, n], recv_sem=grs.at[kind, n],
+            device_id=device, device_id_type=MESH,
+        )
+
+    def tile_at(n):
+        return pl.ds(pl.multiple_of(n * TILE, TILE), TILE)
+
+    def gram_twin(n):
+        return tile_copy(0, n, GP.at[1 - c, :, tile_at(n)], GC.at[:, tile_at(n)], twin)
+
+    def gram_ring(n):
+        return [tile_copy(k, n, GP.at[c, pl.ds(pl.multiple_of(((x + k) % 4) * 64, 64), 64), tile_at(n)],
+                          GX.at[k - 1, :, tile_at(n)], ring[k]) for k in (1, 2, 3)]
+
+    def gram_other(n):
+        rows = pl.ds(pl.multiple_of((1 - a) * 32, 32), 32)
+        return tile_copy(4, n, GT.at[rows, tile_at(n)], GD.at[:, tile_at(n)], other)
 
     def gram_rows(last):
         slabs = [chunk_of(i) for i in ((6, 7) if last else range(6))]
@@ -210,17 +232,18 @@
             PKT[group * 128 : (group + 1) * 128, 0:count] = picked.astype(BF16)
 
         def gram_tile(n, _):
-            at = pl.ds(pl.multiple_of(n * 256, 256), 256)
+            at = pl.ds(pl.multiple_of(n * TILE, TILE), TILE)
             tile = dot(PKT[:, 0:count], jnp.concatenate([X[g, :, at] for g in slabs], axis=0))
             if last:
                 GP[0, :, at] = (tile[0:256] + S0[:, at]).astype(BF16)
                 GP[1, :, at] = (tile[256:512] + S1[:, at]).astype(BF16)
+                gram_twin(n).start()
             else:
                 S0[:, at] = tile[0:256]
                 S1[:, at] = tile[256:512]
             return 0
 
-        lax.fori_loop(0, 16, gram_tile, 0)
+        lax.fori_loop(0, D // TILE, gram_tile, 0)
 
     def gather_stage(stage, _):
         @pl.when(stage == 0)
@@ -251,34 +274,39 @@
             for copy in y_near:
                 copy.wait_recv()
 
-        @pl.when(stage == 3)
-        def _():
-            gram_rows(False)
-            for copy in (*half_first, *half_next, *y_oppo):
+        project((2 * stage, 2 * stage + 1))
+
+        @pl.when(stage > 0)
+        def _():
+            forward_kv((2 * stage - 2, 2 * stage - 1))
+
+        return 0
+
+    lax.fori_loop(0, 3, gather_stage, 0)
+    gram_rows(False)
+    forward_kv((4, 5))
+
+    def gather_last(i, _):
+        @pl.when(i == 0)
+        def _():
+            for copy in half_first:
                 copy.wait_recv()
 
-        project(stage)
-
-        @pl.when(stage > 0)
-        def _():
-            forward_kv(stage - 1)
-
-        return 0
-
-    lax.fori_loop(0, 4, gather_stage, 0)
+        @pl.when(i == 1)
+        def _():
+            for copy in (*half_next, *y_oppo):
+                copy.wait_recv()
+
+        project((6 + i,))
+        return 0
+
+    lax.fori_loop(0, 2, gather_last, 0)
+    forward_kv((6,))
 
     wo_far.wait_recv()
     wo_twin.start()
     gram_rows(True)
-    gram_twin = send(20, GP.at[1 - c], GC, twin)
-    gram_twin.start()
-    gram_ring = [None] + [
-        send(20 + k, GP.at[c, pl.ds(pl.multiple_of(((x + k) % 4) * 64, 64), 64)], GX.at[k - 1], ring[k])
-        for k in (1, 2, 3)
-    ]
-    gram_other = send(24, GC.at[pl.ds(pl.multiple_of((1 - a) * 32, 32), 32)], GD, other)
-
-    forward_kv(3)
+    forward_kv((7,))
 
     def settle(i, _):
         kv_copy(0, i).wait_recv()
@@ -293,7 +321,7 @@
     late = lax.broadcasted_iota(jnp.int32, (256, HD), 0) % 64 - lax.broadcasted_iota(jnp.int32, (256, HD), 1)
     blank = jnp.zeros((256 - KROWS, HD), BF16)
     ones = jnp.ones((HD, HD), BF16)
-    steps = jnp.minimum(4, b + 1)
+    steps = jnp.minimum(32 // SPAN, (8 * b + 7 + SPAN) // SPAN)
 
     def rows_of(half):
         return pl.ds(pl.multiple_of(half * 256, 256), 256)
@@ -310,12 +338,12 @@
         MX[...] = scores
 
     def score_step(g, half, S, MX, t):
-        first = b * 8 + g + PAD - 8 * (t + 1)
-        keys = jnp.concatenate([keys_of(first + j) for j in range(8)], axis=1)
+        first = b * 8 + g + PAD - SPAN * (t + 1)
+        keys = jnp.concatenate([keys_of(first + j) for j in range(SPAN)], axis=1)
         scores = dot(QE[g, rows_of(half), :], keys)
-        S[:, pl.ds(pl.multiple_of(t * 1024, 1024), 1024)] = scores
+        S[:, pl.ds(pl.multiple_of(t * SPAN * HD, SPAN * HD), SPAN * HD)] = scores
         top = MX[...]
-        for j in range(8):
+        for j in range(SPAN):
             top = jnp.maximum(top, scores[:, j * HD : (j + 1) * HD])
         MX[...] = top
 
@@ -326,12 +354,12 @@
         ACC[...] = dot(probs, values_of(b * 8 + g + PAD))
 
     def mix_step(g, S, t):
-        first = b * 8 + g + PAD - 8 * (t + 1)
-        values = jnp.concatenate([values_of(first + j) for j in range(8)], axis=0)
-        scores = S[:, pl.ds(pl.multiple_of(t * 1024, 1024), 1024)]
+        first = b * 8 + g + PAD - SPAN * (t + 1)
+        values = jnp.concatenate([values_of(first + j) for j in range(SPAN)], axis=0)
+        scores = S[:, pl.ds(pl.multiple_of(t * SPAN * HD, SPAN * HD), SPAN * HD)]
         top = TOP[...]
         probs = jnp.concatenate(
-            [jnp.exp2(scores[:, j * HD : (j + 1) * HD] - top).astype(BF16) for j in range(8)], axis=1)
+            [jnp.exp2(scores[:, j * HD : (j + 1) * HD] - top).astype(BF16) for j in range(SPAN)], axis=1)
         ACC[...] += dot(probs, values)
 
     def mix_last(g, half):
@@ -376,6 +404,27 @@
             recv_sem=swr.at[k, second], device_id=side, device_id_type=MESH,
         )
 
+    def gram_cores():
+        def add(n, _):
+            gram_twin(n).wait_recv()
+            at = tile_at(n)
+            GP[c, :, at] = (GP[c, :, at].astype(F32) + GC[:, at].astype(F32)).astype(BF16)
+            for copy in gram_ring(n):
+                copy.start()
+            return 0
+
+        lax.fori_loop(0, D // TILE, add, 0)
+
+    def gram_quads(n):
+        for copy in gram_ring(n):
+            copy.wait_recv()
+        at = tile_at(n)
+        total = GP[c, pl.ds(pl.multiple_of(x * 64, 64), 64), at].astype(F32)
+        for i in range(3):
+            total = total + GX[i, :, at].astype(F32)
+        GT[:, at] = total.astype(BF16)
+        gram_other(n).start()
+
     def out_stage(k, _):
         rows = [part_of(k, 0), part_of(k, 1)]
 
@@ -396,6 +445,14 @@
             def _():
                 swap(k, 1).start()
 
+            @pl.when((i == 0) & (k == 0))
+            def _():
+                gram_cores()
+
+            @pl.when((k == 1) | (k == 2))
+            def _():
+                gram_quads(2 * k - 2 + i)
+
             return 0
 
         lax.fori_loop(0, 2, unit, 0)
@@ -405,26 +462,16 @@
             [AT[y * 4 + row, pl.ds(pl.multiple_of(half * 64, 64), 64), :] for row, half in rows], axis=0)
 
         def out_tile(n, _):
-            at = pl.ds(pl.multiple_of(n * 512, 512), 512)
+            at = pl.ds(pl.multiple_of(n * OUT, OUT), OUT)
             PT[k, :, at] = (dot(own, WO[0, :, at]) + dot(AR[k], WO[1, :, at])).astype(BF16)
             return 0
 
-        lax.fori_loop(0, 8, out_tile, 0)
+        lax.fori_loop(0, D // OUT, out_tile, 0)
 
         @pl.when(k == 0)
         def _():
             turned[0].start()
             turned[1].start()
-            gram_twin.wait_recv()
-
-            def add(n, _):
-                at = pl.ds(pl.multiple_of(n * 512, 512), 512)
-                GP[c, :, at] = (GP[c, :, at].astype(F32) + GC[:, at].astype(F32)).astype(BF16)
-                return 0
-
-            lax.fori_loop(0, 8, add, 0)
-            for k in (1, 2, 3):
-                gram_ring[k].start()
 
         @pl.when(k == 1)
         def _():
@@ -439,22 +486,6 @@
                 PT[2, at] = (PT[2, at].astype(F32) + RA[which].astype(F32)).astype(BF16)
                 turned[4 + which].start()
 
-        @pl.when(k == 2)
-        def _():
-            for k in (1, 2, 3):
-                gram_ring[k].wait_recv()
-
-            def add(n, _):
-                at = pl.ds(pl.multiple_of(n * 512, 512), 512)
-                total = GP[c, pl.ds(pl.multiple_of(x * 64, 64), 64), at].astype(F32)
-                for k in range(3):
-                    total = total + GX[k, :, at].astype(F32)
-                GC[0:64, at] = total.astype(BF16)
-                return 0
-
-            lax.fori_loop(0, 8, add, 0)
-            gram_other.start()
-
         return 0
 
     start_g = (1 - y) * 4 + zo
@@ -466,15 +497,15 @@
 
     lax.fori_loop(0, steps, start_step, 0)
     lax.fori_loop(0, 4, out_stage, 0)
-    gram_other.wait_recv()
     mine = pl.ds(pl.multiple_of(a * 32, 32), 32)
-    gram[...] = GC[mine, :].astype(F32) + GD[...].astype(F32)
+    for n in range(D // TILE):
+        gram_other(n).wait_recv()
+    gram[...] = GT[mine, :].astype(F32) + GD[...].astype(F32)
     for copy in turned[2:]:
         copy.wait_recv()
-    out[...] = PT[3].astype(F32) + RF[0].astype(F32) + RF[1].astype(F32)
-
-    for copy in [*gathers, wo_far, wo_twin, gram_twin,
-                 *gram_ring[1:], gram_other, *turned]:
+    out[...] = (PT[3].astype(F32) + RF[0].astype(F32) + RF[1].astype(F32)).astype(BF16)
+
+    for copy in [*gathers, wo_far, wo_twin, *turned]:
         copy.wait_send()
 
     def drain(i, _):
@@ -484,12 +515,24 @@
 
     lax.fori_loop(0, 8, drain, 0)
 
+    def drain_gram(n, _):
+        for copy in (gram_twin(n), *gram_ring(n), gram_other(n)):
+            copy.wait_send()
+        return 0
+
+    lax.fori_loop(0, D // TILE, drain_gram, 0)
+
     def drain_swap(k, _):
         swap(k, 0).wait_send()
         swap(k, 1).wait_send()
         return 0
 
     lax.fori_loop(0, 4, drain_swap, 0)
+
+
+def finish(delta, gram, delta_out, gram_out):
+    delta_out[...] = delta[...]
+    gram_out[...] = gram[...] * (1.0 / 16384.0)
 
 
 def per_device(tokens, norm_gain, segment_ids, w_query, w_key, w_value, w_out):
@@ -507,6 +550,7 @@
         pltpu.VMEM((2, 256, D), BF16),
         pltpu.VMEM((256, D), BF16),
         pltpu.VMEM((3, 64, D), BF16),
+        pltpu.VMEM((64, D), BF16),
         pltpu.VMEM((32, D), BF16),
         pltpu.VMEM((8, ROWS, 512), BF16),
         pltpu.VMEM((4, ROWS, 512), BF16),
@@ -525,11 +569,13 @@
         dma((5, 8)),
         dma((4, 2)),
         dma((4, 2)),
+        dma((5, 4)),
+        dma((5, 4)),
         dma((4,)),
     ]
     delta, gram = pl.pallas_call(
         kernel,
-        out_shape=(jax.ShapeDtypeStruct((ROWS, D), F32), jax.ShapeDtypeStruct((32, D), F32)),
+        out_shape=(jax.ShapeDtypeStruct((ROWS, D), BF16), jax.ShapeDtypeStruct((32, D), F32)),
         in_specs=[vmem, vmem, vmem, hbm, hbm, hbm, hbm, vmem, vmem, vmem, vmem],
         out_specs=(vmem, vmem),
         scratch_shapes=scratch,
@@ -538,7 +584,14 @@
         name="sublayer",
     )(tokens[0], norm_gain[None], segment_ids, w_query, w_key, w_value, w_out,
       *[jnp.asarray(t) for t in tables()])
-    return delta.astype(BF16)[None], gram * (1.0 / 16384.0)
+    delta, gram = pl.pallas_call(
+        finish,
+        out_shape=(jax.ShapeDtypeStruct((ROWS, D), BF16), jax.ShapeDtypeStruct((32, D), F32)),
+        in_specs=[vmem, vmem],
+        out_specs=(vmem, vmem),
+        name="finish",
+    )(delta, gram)
+    return delta[None], gram
 
 
 def solution(mesh):

time: 135 us -> 124 us (0.919)
  Pallas kernels: 129 us -> 123 us
  other arithmetic: 4.56 us -> 0 us
    pallas_call x1 -> x2, Pallas kernels: 129 us -> 123 us  [the longest x1 120 us: per_device(): pl.pallas_call(kernel, out_shape=(jax.ShapeDtypeStruct((ROWS, D), BF16),...]
    broadcast_in_dim x1 -> x0, other arithmetic: 2.69 us -> none  [per_device(): return (delta.astype(BF16)[None], gram * (1.0 / 16384.0))]
    mul x1 -> x0, other arithmetic: 1.87 us -> none  [per_device(): return (delta.astype(BF16)[None], gram * (1.0 / 16384.0))]
where the time goes in v3:
time: 124 us
  Pallas kernels  123 us (99%)
    pallas_call x1, Pallas kernels, per_device(): pl.pallas_call(kernel, out_shape=(jax.ShapeDtypeStruct((ROWS, D), BF16),...  120 us
    pallas_call x1, Pallas kernels, per_device(): pl.pallas_call(finish, out_shape=(jax.ShapeDtypeStruct((ROWS, D), BF16),...  2.6 us

profile of v3, /device:TPU:1, one launch (start us, length us, event | category | flops | bytes accessed | tf_op | source)
XLA Modules:
  0.0 123.6 jit_solution(13559093446951708730)
XLA Ops:
  0.6 120.4 %sublayer.1 = (bf16[128,4096]{1,0:T(8,128)(2,1)}, f32[32,4096]{1,0:T(8,128)}) custom-call(bf16[128,4096]{1,0:T(8,128)(2,1)} %bitcast.3, f32[1,4096]{1,0:T(1,128)} %bitcast.4, s32[1,128]{1,0:T(1,128)} %seg.1, bf16[4096,512]{1,0:T(8,128)(2,1)} %wq_h.1, bf16[4096,128]{1,0:T(8,128)(2,1)} %wk_h.1, bf16[4096,128]{1,0:T(8,128)(2,1)} %wv_h.1, ...), custom_call_target="tpu_custom_call" | custom-call | tf_op jit(solution)/shard_map/sublayer/pallas_call | solution.py:576
  121.0 2.6 %finish.1 = (bf16[128,4096]{1,0:T(8,128)(2,1)}, f32[32,4096]{1,0:T(8,128)}) custom-call(bf16[128,4096]{1,0:T(8,128)(2,1)} %get-tuple-element.6.delta, f32[32,4096]{1,0:T(8,128)} %get-tuple-element.7.gram), custom_call_target="tpu_custom_call" | custom-call | tf_op jit(solution)/shard_map/finish/pallas_call | solution.py:587

commit v4 on v3

--- a/solution.py
+++ b/solution.py
@@ -18,7 +18,7 @@
 FEATS = 16
 KROWS = HD + FEATS
 SPAN = 16
-OUT = 4096
+OUT = 2048
 TILE = 1024
 PAD = SPAN
 CUT = 18 * 128
@@ -40,10 +40,10 @@
 
 
 def kernel(
-    tok, gain, seg, wq_h, wk_h, wv_h, wo_h, base_cos, base_sin, step_cos, step_sin,
+    tok_h, gain, seg, wq_h, wk_h, wv_h, wo_h, base_cos, base_sin, step_cos, step_sin,
     out, gram,
-    X, WQ, WKV, WO, QE, KV, PKT, GP, GC, GX, GT, GD, AT, AR, PT, RA, RF, ACC, TOP, S0, S1, M0, M1,
-    ss, rs, kss, krs, sws, swr, gss, grs, ls,
+    X, E, tok, WQ, WKV, WO, QE, KV, PKT, GP, GC, GX, GT, GD, AT, AR, PT, RA, RF, ACC, TOP, S0, S1, M0, M1,
+    ss, rs, kss, krs, sws, swr, gss, grs, ess, ers, tss, trs, ls,
 ):
     a, b, h = lax.axis_index("dp"), lax.axis_index("blk"), lax.axis_index("heads")
     x, c = b // 2, b % 2
@@ -56,19 +56,23 @@
     other = (1 - a, b, h)
     ring = [None] + [(a, ((x + k) % 4) * 2 + c, h) for k in (1, 2, 3)]
 
+    load_tok = pltpu.make_async_copy(tok_h, tok, ls.at[4])
+    load_tok.start()
     loads = [
         pltpu.make_async_copy(wk_h, WKV.at[:, 0:HD], ls.at[0]),
         pltpu.make_async_copy(wv_h, WKV.at[:, HD : 2 * HD], ls.at[1]),
         pltpu.make_async_copy(wq_h, WQ, ls.at[2]),
         pltpu.make_async_copy(wo_h, WO.at[0], ls.at[3]),
     ]
+    barrier = pltpu.get_barrier_semaphore()
+    group = [(a, b, ((y + j // 4) % 2) * 4 + (z + j) % 4) for j in range(1, 8)]
+    partners = group + [far, twin, other] + ring[1:]
+    for partner in partners:
+        pl.semaphore_signal(barrier, inc=1, device_id=partner, device_id_type=MESH)
+
+    load_tok.wait()
     for load in loads:
         load.start()
-
-    barrier = pltpu.get_barrier_semaphore()
-    partners = [up, down, side, far, twin, other] + ring[1:]
-    for partner in partners:
-        pl.semaphore_signal(barrier, inc=1, device_id=partner, device_id_type=MESH)
 
     def normalise(i, _):
         at = pl.ds(pl.multiple_of(i * 16, 16), 16)
@@ -78,8 +82,8 @@
         return 0
 
     lax.fori_loop(0, ROWS // 16, normalise, 0)
-    feature = lax.broadcasted_iota(jnp.int32, (ROWS, ROWS), 0)
-    X[h, :, D : D + ROWS] = jnp.where(feature == seg[...], 1.0, 0.0).astype(BF16)
+    feature = lax.broadcasted_iota(jnp.int32, (FEATS, ROWS), 0)
+    E[h] = jnp.where(feature == seg[...], 1.0, 0.0).astype(BF16)
 
     pl.semaphore_wait(barrier, len(partners))
 
@@ -89,7 +93,7 @@
             device_id=device, device_id_type=MESH,
         )
 
-    FIRST, LAST = pl.ds(0, CUT), pl.ds(CUT, D + ROWS - CUT)
+    FIRST, LAST = pl.ds(0, CUT), pl.ds(CUT, D - CUT)
 
     def move(i, g, columns, device, half=None):
         rows = pl.ds(0, ROWS) if half is None else pl.ds(half * 64, 64)
@@ -110,6 +114,15 @@
     half_next = [move(16, nm, FIRST, up, 0), move(17, np_, FIRST, down, 1)]
     gathers = [y_first, y_last, *z_first, *z_last, *n_first, *half_first, *half_last, *y_near, *y_oppo, *half_next]
     for copy in (y_first, *z_last, *z_first, y_last):
+        copy.start()
+    ids = [
+        pltpu.make_async_remote_copy(
+            src_ref=E.at[h], dst_ref=E.at[h], send_sem=ess.at[j], recv_sem=ers.at[j],
+            device_id=device, device_id_type=MESH,
+        )
+        for j, device in enumerate(group)
+    ]
+    for copy in ids:
         copy.start()
     half_rows = pl.ds(pl.multiple_of(c * 256, 256), 256)
     wo_far = send(18, wo_h.at[half_rows], WO.at[1, half_rows], far)
@@ -162,7 +175,7 @@
             key = kv[k * ROWS : (k + 1) * ROWS, 0:HD]
             key = key * cosine + pltpu.roll(key, 64, 1) * sine
             KV[slot, 0:HD, :] = key.T.astype(BF16)
-            KV[slot, HD:KROWS, :] = X[g, 0:FEATS, D : D + ROWS]
+            KV[slot, HD:KROWS, :] = E[g]
             KV[slot, KROWS : KROWS + HD, :] = kv[k * ROWS : (k + 1) * ROWS, HD : 2 * HD].astype(BF16)
         for i in items:
             for kind in range(3):
@@ -178,7 +191,7 @@
                         at = half * 256 + (n * 2 + m) * 64
                         QE[g, at : at + 64, 0:HD] = head[half * 64 : half * 64 + 64].astype(BF16)
         for g in pair:
-            mine = X[g, :, D : D + ROWS].astype(F32).T
+            mine = jnp.concatenate([E[g].astype(F32), jnp.zeros((ROWS - FEATS, ROWS), F32)], axis=0).T
             ext = jnp.where(lane < 8, jnp.where(mine > 0.5, 0.0, -BIG), jnp.where(lane == 8, -BIG, 0.0))
             for m in range(8):
                 at = (m // 4) * 64
@@ -259,6 +272,8 @@
                 z_first[k].wait_recv()
                 half_first[k].start()
             y_last.wait_recv()
+            for copy in ids:
+                copy.wait_recv()
 
         @pl.when(stage == 1)
         def _():
@@ -381,14 +396,18 @@
         mix_last(g, half)
 
     top, low = pl.ds(0, 64), pl.ds(64, 64)
-    turned = [
-        send(25, PT.at[0, top], RA.at[0], up),
-        send(26, PT.at[0, low], RA.at[1], down),
-        send(27, PT.at[1, top], RF.at[0, low], up),
-        send(28, PT.at[1, low], RF.at[1, top], down),
-        send(29, PT.at[2, top], RF.at[0, top], up),
-        send(30, PT.at[2, low], RF.at[1, low], down),
-    ]
+
+    def turned(kind, n):
+        at = pl.ds(pl.multiple_of(n * OUT, OUT), OUT)
+        src = PT.at[kind // 2, low if kind % 2 else top, at]
+        dst = [
+            RA.at[0, :, at], RA.at[1, :, at], RF.at[0, low, at],
+            RF.at[1, top, at], RF.at[0, top, at], RF.at[1, low, at],
+        ][kind]
+        return pltpu.make_async_remote_copy(
+            src_ref=src, dst_ref=dst, send_sem=tss.at[kind, n], recv_sem=trs.at[kind, n],
+            device_id=down if kind % 2 else up, device_id_type=MESH,
+        )
 
     def part_of(k, second):
         row = jnp.where(k == 0, zo, jnp.where(k == 3, z, jnp.where(second == 0, zp, zm)))
@@ -463,29 +482,28 @@
 
         def out_tile(n, _):
             at = pl.ds(pl.multiple_of(n * OUT, OUT), OUT)
-            PT[k, :, at] = (dot(own, WO[0, :, at]) + dot(AR[k], WO[1, :, at])).astype(BF16)
+            part = dot(own, WO[0, :, at]) + dot(AR[k], WO[1, :, at])
+
+            @pl.when(k != 2)
+            def _():
+                PT[k, :, at] = part.astype(BF16)
+
+            @pl.when(k == 2)
+            def _():
+                for which, rows in enumerate((top, low)):
+                    turned(which, n).wait_recv()
+                    first = 64 * which
+                    PT[2, rows, at] = (part[first : first + 64] + RA[which, :, at].astype(F32)).astype(BF16)
+
+            for stage in range(3):
+                @pl.when(k == stage)
+                def _(stage=stage):
+                    turned(2 * stage, n).start()
+                    turned(2 * stage + 1, n).start()
+
             return 0
 
         lax.fori_loop(0, D // OUT, out_tile, 0)
-
-        @pl.when(k == 0)
-        def _():
-            turned[0].start()
-            turned[1].start()
-
-        @pl.when(k == 1)
-        def _():
-            turned[2].start()
-            turned[3].start()
-
-        @pl.when(k == 2)
-        def _():
-            for which in (0, 1):
-                turned[which].wait_recv()
-                at = pl.ds(64 * which, 64)
-                PT[2, at] = (PT[2, at].astype(F32) + RA[which].astype(F32)).astype(BF16)
-                turned[4 + which].start()
-
         return 0
 
     start_g = (1 - y) * 4 + zo
@@ -501,11 +519,17 @@
     for n in range(D // TILE):
         gram_other(n).wait_recv()
     gram[...] = GT[mine, :].astype(F32) + GD[...].astype(F32)
-    for copy in turned[2:]:
-        copy.wait_recv()
-    out[...] = (PT[3].astype(F32) + RF[0].astype(F32) + RF[1].astype(F32)).astype(BF16)
-
-    for copy in [*gathers, wo_far, wo_twin, *turned]:
+
+    def total(n, _):
+        at = pl.ds(pl.multiple_of(n * OUT, OUT), OUT)
+        for kind in range(2, 6):
+            turned(kind, n).wait_recv()
+        out[:, at] = (PT[3, :, at].astype(F32) + RF[0, :, at].astype(F32) + RF[1, :, at].astype(F32)).astype(BF16)
+        return 0
+
+    lax.fori_loop(0, D // OUT, total, 0)
+
+    for copy in [*gathers, *ids, wo_far, wo_twin]:
         copy.wait_send()
 
     def drain(i, _):
@@ -519,6 +543,13 @@
         for copy in (gram_twin(n), *gram_ring(n), gram_other(n)):
             copy.wait_send()
         return 0
+
+    def drain_turned(n, _):
+        for kind in range(6):
+            turned(kind, n).wait_send()
+        return 0
+
+    lax.fori_loop(0, D // OUT, drain_turned, 0)
 
     lax.fori_loop(0, D // TILE, drain_gram, 0)
 
@@ -540,7 +571,9 @@
     hbm = pl.BlockSpec(memory_space=pl.ANY)
     dma = pltpu.SemaphoreType.DMA
     scratch = [
-        pltpu.VMEM((8, ROWS, D + ROWS), BF16),
+        pltpu.VMEM((8, ROWS, D), BF16),
+        pltpu.VMEM((8, FEATS, ROWS), BF16),
+        pltpu.VMEM((ROWS, D), BF16),
         pltpu.VMEM((D, 512), BF16),
         pltpu.VMEM((D, 256), BF16),
         pltpu.VMEM((2, 512, D), BF16),
@@ -571,12 +604,16 @@
         dma((4, 2)),
         dma((5, 4)),
         dma((5, 4)),
-        dma((4,)),
+        dma((7,)),
+        dma((7,)),
+        dma((6, 2)),
+        dma((6, 2)),
+        dma((5,)),
     ]
     delta, gram = pl.pallas_call(
         kernel,
         out_shape=(jax.ShapeDtypeStruct((ROWS, D), BF16), jax.ShapeDtypeStruct((32, D), F32)),
-        in_specs=[vmem, vmem, vmem, hbm, hbm, hbm, hbm, vmem, vmem, vmem, vmem],
+        in_specs=[hbm, vmem, vmem, hbm, hbm, hbm, hbm, vmem, vmem, vmem, vmem],
         out_specs=(vmem, vmem),
         scratch_shapes=scratch,
         compiler_params=pltpu.CompilerParams(

time: 124 us -> 122 us (0.984)
  Pallas kernels: 123 us -> 121 us
    pallas_call x1, Pallas kernels: 120 us -> 118 us  [per_device(): pl.pallas_call(kernel, out_shape=(jax.ShapeDtypeStruct((ROWS, D), BF16),...]
where the time goes in v4:
time: 122 us; the launch traced here: 121 us
  Pallas kernels  121 us (99%)
    pallas_call x1, Pallas kernels, per_device(): pl.pallas_call(kernel, out_shape=(jax.ShapeDtypeStruct((ROWS, D), BF16),...  118 us
    pallas_call x1, Pallas kernels, per_device(): pl.pallas_call(finish, out_shape=(jax.ShapeDtypeStruct((ROWS, D), BF16),...  2.6 us

profile of v4, /device:TPU:1, one launch (start us, length us, event | category | flops | bytes accessed | tf_op | source)
XLA Modules:
  0.0 121.3 jit_solution(14691428158375281834)
XLA Ops:
  0.6 118.0 %sublayer.1 = (bf16[128,4096]{1,0:T(8,128)(2,1)}, f32[32,4096]{1,0:T(8,128)}) custom-call(bf16[128,4096]{1,0:T(8,128)(2,1)} %bitcast.3, f32[1,4096]{1,0:T(1,128)} %bitcast.4, s32[1,128]{1,0:T(1,128)} %seg.1, bf16[4096,512]{1,0:T(8,128)(2,1)} %wq_h.1, bf16[4096,128]{1,0:T(8,128)(2,1)} %wk_h.1, bf16[4096,128]{1,0:T(8,128)(2,1)} %wv_h.1, ...), custom_call_target="tpu_custom_call" | custom-call | tf_op jit(solution)/shard_map/sublayer/pallas_call | solution.py:613
  118.7 2.6 %finish.1 = (bf16[128,4096]{1,0:T(8,128)(2,1)}, f32[32,4096]{1,0:T(8,128)}) custom-call(bf16[128,4096]{1,0:T(8,128)(2,1)} %get-tuple-element.6.delta, f32[32,4096]{1,0:T(8,128)} %get-tuple-element.7.gram), custom_call_target="tpu_custom_call" | custom-call | tf_op jit(solution)/shard_map/finish/pallas_call | solution.py:624

commit v5 on v4

--- a/solution.py
+++ b/solution.py
@@ -43,7 +43,7 @@
     tok_h, gain, seg, wq_h, wk_h, wv_h, wo_h, base_cos, base_sin, step_cos, step_sin,
     out, gram,
     X, E, tok, WQ, WKV, WO, QE, KV, PKT, GP, GC, GX, GT, GD, AT, AR, PT, RA, RF, ACC, TOP, S0, S1, M0, M1,
-    ss, rs, kss, krs, sws, swr, gss, grs, ess, ers, tss, trs, ls,
+    ss, rs, kss, krs, sws, swr, gss, grs, ess, ers, tss, trs, ras, rar, ls,
 ):
     a, b, h = lax.axis_index("dp"), lax.axis_index("blk"), lax.axis_index("heads")
     x, c = b // 2, b % 2
@@ -187,15 +187,15 @@
                 for m in range(2):
                     head = part[k * ROWS : (k + 1) * ROWS, m * HD : (m + 1) * HD]
                     head = (head * cosine + pltpu.roll(head, 64, 1) * sine) * scale
-                    for half in range(2):
-                        at = half * 256 + (n * 2 + m) * 64
-                        QE[g, at : at + 64, 0:HD] = head[half * 64 : half * 64 + 64].astype(BF16)
+                    for part_at in range(4):
+                        at = part_at * 128 + (n * 2 + m) * 32
+                        QE[g, at : at + 32, 0:HD] = head[part_at * 32 : part_at * 32 + 32].astype(BF16)
         for g in pair:
             mine = jnp.concatenate([E[g].astype(F32), jnp.zeros((ROWS - FEATS, ROWS), F32)], axis=0).T
             ext = jnp.where(lane < 8, jnp.where(mine > 0.5, 0.0, -BIG), jnp.where(lane == 8, -BIG, 0.0))
-            for m in range(8):
-                at = (m // 4) * 64
-                QE[g, m * 64 : m * 64 + 64, HD : 2 * HD] = ext[at : at + 64].astype(BF16)
+            for m in range(16):
+                at = (m // 4) * 32
+                QE[g, m * 32 : m * 32 + 32, HD : 2 * HD] = ext[at : at + 32].astype(BF16)
 
     def forward_kv(items):
         for i in items:
@@ -323,6 +323,19 @@
     gram_rows(True)
     forward_kv((7,))
 
+    def gram_cores():
+        def add(n, _):
+            gram_twin(n).wait_recv()
+            at = tile_at(n)
+            GP[c, :, at] = (GP[c, :, at].astype(F32) + GC[:, at].astype(F32)).astype(BF16)
+            for copy in gram_ring(n):
+                copy.start()
+            return 0
+
+        lax.fori_loop(0, D // TILE, add, 0)
+
+    gram_cores()
+
     def settle(i, _):
         kv_copy(0, i).wait_recv()
         kv_copy(3, i).wait_recv()
@@ -333,13 +346,16 @@
     wo_twin.wait_recv()
     loads[3].wait()
 
-    late = lax.broadcasted_iota(jnp.int32, (256, HD), 0) % 64 - lax.broadcasted_iota(jnp.int32, (256, HD), 1)
+    row_in = lax.broadcasted_iota(jnp.int32, (256, HD), 0)
+    late = row_in % 32 - lax.broadcasted_iota(jnp.int32, (256, HD), 1)
+    second_quarter = row_in >= 128
     blank = jnp.zeros((256 - KROWS, HD), BF16)
     ones = jnp.ones((HD, HD), BF16)
     steps = jnp.minimum(32 // SPAN, (8 * b + 7 + SPAN) // SPAN)
 
-    def rows_of(half):
-        return pl.ds(pl.multiple_of(half * 256, 256), 256)
+    def queries_of(g, quarters):
+        return jnp.concatenate(
+            [QE[g, pl.ds(pl.multiple_of(q * 128, 128), 128), :] for q in quarters], axis=0)
 
     def keys_of(slot):
         return jnp.concatenate([KV[slot, 0:KROWS, :], blank], axis=0)
@@ -348,14 +364,15 @@
         return jnp.concatenate([KV[slot, KROWS : KROWS + HD, :], ones], axis=1)
 
     def score_first(g, half, S, MX):
-        scores = jnp.where(late + half * 64 >= 0, dot(QE[g, rows_of(half), :], keys_of(b * 8 + g + PAD)), -BIG)
+        scores = jnp.where(late + jnp.where(second_quarter, half[1], half[0]) * 32 >= 0,
+                           dot(queries_of(g, half), keys_of(b * 8 + g + PAD)), -BIG)
         S[:, WINDOW : WINDOW + HD] = scores
         MX[...] = scores
 
     def score_step(g, half, S, MX, t):
         first = b * 8 + g + PAD - SPAN * (t + 1)
         keys = jnp.concatenate([keys_of(first + j) for j in range(SPAN)], axis=1)
-        scores = dot(QE[g, rows_of(half), :], keys)
+        scores = dot(queries_of(g, half), keys)
         S[:, pl.ds(pl.multiple_of(t * SPAN * HD, SPAN * HD), SPAN * HD)] = scores
         top = MX[...]
         for j in range(SPAN):
@@ -377,13 +394,14 @@
             [jnp.exp2(scores[:, j * HD : (j + 1) * HD] - top).astype(BF16) for j in range(SPAN)], axis=1)
         ACC[...] += dot(probs, values)
 
-    def mix_last(g, half):
+    def mix_last(place):
         mixed = (ACC[:, 0:HD] / ACC[:, HD : 2 * HD]).astype(BF16)
-        rows = pl.ds(pl.multiple_of(half * 64, 64), 64)
-        for m in range(4):
-            AT[g, rows, m * HD : (m + 1) * HD] = mixed[m * 64 : m * 64 + 64]
-
-    def both(g, half, S, MX, next_g, next_half, next_S, next_MX):
+        own, k, second = place
+        for m in range(8):
+            rows = pl.ds(pl.multiple_of(second * 64 + (m // 4) * 32, 32), 32)
+            AT[own * 4 + k, rows, (m % 4) * HD : (m % 4 + 1) * HD] = mixed[m * 32 : m * 32 + 32]
+
+    def both(g, place, S, MX, next_g, next_half, next_S, next_MX):
         mix_first(g, S, MX)
         score_first(next_g, next_half, next_S, next_MX)
 
@@ -393,46 +411,41 @@
             return 0
 
         lax.fori_loop(0, steps, step, 0)
-        mix_last(g, half)
+        mix_last(place)
 
     top, low = pl.ds(0, 64), pl.ds(64, 64)
 
     def turned(kind, n):
         at = pl.ds(pl.multiple_of(n * OUT, OUT), OUT)
-        src = PT.at[kind // 2, low if kind % 2 else top, at]
-        dst = [
-            RA.at[0, :, at], RA.at[1, :, at], RF.at[0, low, at],
-            RF.at[1, top, at], RF.at[0, top, at], RF.at[1, low, at],
-        ][kind]
+        src = PT.at[1 + kind // 2, low if kind % 2 else top, at]
+        dst = [RF.at[0, low, at], RF.at[1, top, at], RF.at[0, top, at], RF.at[1, low, at]][kind]
         return pltpu.make_async_remote_copy(
             src_ref=src, dst_ref=dst, send_sem=tss.at[kind, n], recv_sem=trs.at[kind, n],
             device_id=down if kind % 2 else up, device_id_type=MESH,
         )
 
+    def relayed(which, second, n):
+        at = pl.ds(pl.multiple_of(n * OUT, OUT), OUT)
+        rows = pl.ds(pl.multiple_of(second * 64 + which * 32, 32), 32)
+        to = pl.ds(pl.multiple_of(second * 32, 32), 32)
+        return pltpu.make_async_remote_copy(
+            src_ref=PT.at[0, rows, at], dst_ref=RA.at[which, to, at], send_sem=ras.at[which, second, n],
+            recv_sem=rar.at[which, second, n], device_id=down if which else up, device_id_type=MESH,
+        )
+
     def part_of(k, second):
         row = jnp.where(k == 0, zo, jnp.where(k == 3, z, jnp.where(second == 0, zp, zm)))
-        half = jnp.where(k == 1, 1 - second, second)
-        return row, half
+        odd = jnp.where(k == 1, 1 - second, second)
+        mixed = (k == 1) | (k == 2)
+        first = jnp.where(mixed, odd, 2 * second)
+        return row, (first, first + jnp.where(mixed, 2, 1))
 
     def swap(k, second):
-        row, half = part_of(k, second)
-        rows = pl.ds(pl.multiple_of(half * 64, 64), 64)
-        to = pl.ds(pl.multiple_of(second * 64, 64), 64)
+        rows = pl.ds(pl.multiple_of(second * 64, 64), 64)
         return pltpu.make_async_remote_copy(
-            src_ref=AT.at[(1 - y) * 4 + row, rows], dst_ref=AR.at[k, to], send_sem=sws.at[k, second],
+            src_ref=AT.at[k, rows], dst_ref=AR.at[k, rows], send_sem=sws.at[k, second],
             recv_sem=swr.at[k, second], device_id=side, device_id_type=MESH,
         )
-
-    def gram_cores():
-        def add(n, _):
-            gram_twin(n).wait_recv()
-            at = tile_at(n)
-            GP[c, :, at] = (GP[c, :, at].astype(F32) + GC[:, at].astype(F32)).astype(BF16)
-            for copy in gram_ring(n):
-                copy.start()
-            return 0
-
-        lax.fori_loop(0, D // TILE, add, 0)
 
     def gram_quads(n):
         for copy in gram_ring(n):
@@ -444,45 +457,36 @@
         GT[:, at] = total.astype(BF16)
         gram_other(n).start()
 
-    def out_stage(k, _):
-        rows = [part_of(k, 0), part_of(k, 1)]
-
-        def unit(i, _):
-            col = jnp.where(i == 0, 1 - y, y) * 4
-            after = jnp.minimum(2 * k + i + 1, 7)
-            after_col = jnp.where(after % 2 == 0, 1 - y, y) * 4
-            after_row, after_half = part_of(after // 2, 0)
-            both(col + rows[0][0], rows[0][1], S0, M0, col + rows[1][0], rows[1][1], S1, M1)
-
-            @pl.when(i == 0)
-            def _():
-                swap(k, 0).start()
-
-            both(col + rows[1][0], rows[1][1], S1, M1, after_col + after_row, after_half, S0, M0)
-
-            @pl.when(i == 0)
-            def _():
-                swap(k, 1).start()
-
-            @pl.when((i == 0) & (k == 0))
-            def _():
-                gram_cores()
-
-            @pl.when((k == 1) | (k == 2))
-            def _():
-                gram_quads(2 * k - 2 + i)
-
+    def item_of(i):
+        k, j = i // 4, i % 4
+        own = jnp.where(k == 0, j % 2, j // 2)
+        second = jnp.where(k == 0, j // 2, j % 2)
+        row, quarters = part_of(k, second)
+        return jnp.where(own == 1, y, 1 - y) * 4 + row, quarters, (own, k, second)
+
+    def project_out(k, rows, n):
+        at = pl.ds(pl.multiple_of(n * OUT, OUT), OUT)
+        return at, dot(AT[4 + k, rows, :], WO[0, :, at]) + dot(AR[k, rows, :], WO[1, :, at])
+
+    def out_first(second):
+        swap(0, second).wait_recv()
+
+        def tile(n, _):
+            rows = pl.ds(pl.multiple_of(second * 64, 64), 64)
+            at, part = project_out(0, rows, n)
+            PT[0, rows, at] = part.astype(BF16)
+            relayed(0, second, n).start()
+            relayed(1, second, n).start()
             return 0
 
-        lax.fori_loop(0, 2, unit, 0)
+        lax.fori_loop(0, D // OUT, tile, 0)
+
+    def out_round(k):
         swap(k, 0).wait_recv()
         swap(k, 1).wait_recv()
-        own = jnp.concatenate(
-            [AT[y * 4 + row, pl.ds(pl.multiple_of(half * 64, 64), 64), :] for row, half in rows], axis=0)
-
-        def out_tile(n, _):
-            at = pl.ds(pl.multiple_of(n * OUT, OUT), OUT)
-            part = dot(own, WO[0, :, at]) + dot(AR[k], WO[1, :, at])
+
+        def tile(n, _):
+            at, part = project_out(k, pl.ds(0, ROWS), n)
 
             @pl.when(k != 2)
             def _():
@@ -491,30 +495,64 @@
             @pl.when(k == 2)
             def _():
                 for which, rows in enumerate((top, low)):
-                    turned(which, n).wait_recv()
+                    relayed(which, 0, n).wait_recv()
+                    relayed(which, 1, n).wait_recv()
                     first = 64 * which
                     PT[2, rows, at] = (part[first : first + 64] + RA[which, :, at].astype(F32)).astype(BF16)
 
-            for stage in range(3):
+            for stage in (1, 2):
                 @pl.when(k == stage)
                 def _(stage=stage):
-                    turned(2 * stage, n).start()
-                    turned(2 * stage + 1, n).start()
+                    turned(2 * stage - 2, n).start()
+                    turned(2 * stage - 1, n).start()
 
             return 0
 
-        lax.fori_loop(0, D // OUT, out_tile, 0)
+        lax.fori_loop(0, D // OUT, tile, 0)
+
+    def item_pair(p, _):
+        g0, quarters0, place0 = item_of(2 * p)
+        g1, quarters1, place1 = item_of(2 * p + 1)
+        g2, quarters2, _place = item_of(jnp.minimum(2 * p + 2, 15))
+        both(g0, place0, S0, M0, g1, quarters1, S1, M1)
+
+        @pl.when((p < 2) | (p % 2 == 0))
+        def _():
+            swap(place0[1], place0[2]).start()
+
+        @pl.when(p == 1)
+        def _():
+            out_first(0)
+
+        both(g1, place1, S1, M1, g2, quarters2, S0, M0)
+
+        @pl.when((p >= 2) & (p % 2 == 0))
+        def _():
+            swap(place1[1], place1[2]).start()
+
+        @pl.when(p == 1)
+        def _():
+            out_first(1)
+
+        @pl.when((p >= 2) & (p < 6))
+        def _():
+            gram_quads(p - 2)
+
+        @pl.when((p >= 2) & (p % 2 == 1))
+        def _():
+            out_round(p // 2)
+
         return 0
 
     start_g = (1 - y) * 4 + zo
-    score_first(start_g, 0, S0, M0)
+    score_first(start_g, (0, 1), S0, M0)
 
     def start_step(t, _):
-        score_step(start_g, 0, S0, M0, t)
+        score_step(start_g, (0, 1), S0, M0, t)
         return 0
 
     lax.fori_loop(0, steps, start_step, 0)
-    lax.fori_loop(0, 4, out_stage, 0)
+    lax.fori_loop(0, 8, item_pair, 0)
     mine = pl.ds(pl.multiple_of(a * 32, 32), 32)
     for n in range(D // TILE):
         gram_other(n).wait_recv()
@@ -522,9 +560,12 @@
 
     def total(n, _):
         at = pl.ds(pl.multiple_of(n * OUT, OUT), OUT)
-        for kind in range(2, 6):
+        for kind in range(4):
             turned(kind, n).wait_recv()
-        out[:, at] = (PT[3, :, at].astype(F32) + RF[0, :, at].astype(F32) + RF[1, :, at].astype(F32)).astype(BF16)
+        for q in range(4):
+            to, given = pl.ds(q * 32, 32), pl.ds((q % 2) * 64 + (q // 2) * 32, 32)
+            out[to, at] = (PT[3, to, at].astype(F32) + RF[0, given, at].astype(F32)
+                           + RF[1, given, at].astype(F32)).astype(BF16)
         return 0
 
     lax.fori_loop(0, D // OUT, total, 0)
@@ -545,8 +586,11 @@
         return 0
 
     def drain_turned(n, _):
-        for kind in range(6):
+        for kind in range(4):
             turned(kind, n).wait_send()
+        for which in range(2):
+            for second in range(2):
+                relayed(which, second, n).wait_send()
         return 0
 
     lax.fori_loop(0, D // OUT, drain_turned, 0)
@@ -606,8 +650,10 @@
         dma((5, 4)),
         dma((7,)),
         dma((7,)),
-        dma((6, 2)),
-        dma((6, 2)),
+        dma((4, 2)),
+        dma((4, 2)),
+        dma((2, 2, 2)),
+        dma((2, 2, 2)),
         dma((5,)),
     ]
     delta, gram = pl.pallas_call(

time: 122 us -> 121 us (level)
  no operation moved by 1% of the time
where the time goes in v5:
time: 121 us
  Pallas kernels  120 us (99%)
    pallas_call x1, Pallas kernels, per_device(): pl.pallas_call(kernel, out_shape=(jax.ShapeDtypeStruct((ROWS, D), BF16),...  118 us
    pallas_call x1, Pallas kernels, per_device(): pl.pallas_call(finish, out_shape=(jax.ShapeDtypeStruct((ROWS, D), BF16),...  2.6 us

profile of v5, /device:TPU:1, one launch (start us, length us, event | category | flops | bytes accessed | tf_op | source)
XLA Modules:
  0.0 120.9 jit_solution(10341709868198997959)
XLA Ops:
  0.6 117.6 %sublayer.1 = (bf16[128,4096]{1,0:T(8,128)(2,1)}, f32[32,4096]{1,0:T(8,128)}) custom-call(bf16[128,4096]{1,0:T(8,128)(2,1)} %bitcast.3, f32[1,4096]{1,0:T(1,128)} %bitcast.4, s32[1,128]{1,0:T(1,128)} %seg.1, bf16[4096,512]{1,0:T(8,128)(2,1)} %wq_h.1, bf16[4096,128]{1,0:T(8,128)(2,1)} %wk_h.1, bf16[4096,128]{1,0:T(8,128)(2,1)} %wv_h.1, ...), custom_call_target="tpu_custom_call" | custom-call | tf_op jit(solution)/shard_map/sublayer/pallas_call | solution.py:659
  118.3 2.6 %finish.1 = (bf16[128,4096]{1,0:T(8,128)(2,1)}, f32[32,4096]{1,0:T(8,128)}) custom-call(bf16[128,4096]{1,0:T(8,128)(2,1)} %get-tuple-element.6.delta, f32[32,4096]{1,0:T(8,128)} %get-tuple-element.7.gram), custom_call_target="tpu_custom_call" | custom-call | tf_op jit(solution)/shard_map/finish/pallas_call | solution.py:670

commit v6 on v5

--- a/solution.py
+++ b/solution.py
@@ -670,8 +670,9 @@
     delta, gram = pl.pallas_call(
         finish,
         out_shape=(jax.ShapeDtypeStruct((ROWS, D), BF16), jax.ShapeDtypeStruct((32, D), F32)),
-        in_specs=[vmem, vmem],
-        out_specs=(vmem, vmem),
+        grid=(2,),
+        in_specs=[pl.BlockSpec((64, D), lambda i: (i, 0)), pl.BlockSpec((16, D), lambda i: (i, 0))],
+        out_specs=(pl.BlockSpec((64, D), lambda i: (i, 0)), pl.BlockSpec((16, D), lambda i: (i, 0))),
         name="finish",
     )(delta, gram)
     return delta[None], gram

time: 121 us -> 121 us (level)
  no operation moved by 1% of the time
where the time goes in v6:
time: 121 us
  Pallas kernels  120 us (99%)
    pallas_call x1, Pallas kernels, per_device(): pl.pallas_call(kernel, out_shape=(jax.ShapeDtypeStruct((ROWS, D), BF16),...  118 us

profile of v6, /device:TPU:1, one launch (start us, length us, event | category | flops | bytes accessed | tf_op | source)
XLA Modules:
  0.0 120.6 jit_solution(6273937169785286629)
XLA Ops:
  0.6 117.6 %sublayer.1 = (bf16[128,4096]{1,0:T(8,128)(2,1)}, f32[32,4096]{1,0:T(8,128)}) custom-call(bf16[128,4096]{1,0:T(8,128)(2,1)} %bitcast.3, f32[1,4096]{1,0:T(1,128)} %bitcast.4, s32[1,128]{1,0:T(1,128)} %seg.1, bf16[4096,512]{1,0:T(8,128)(2,1)} %wq_h.1, bf16[4096,128]{1,0:T(8,128)(2,1)} %wk_h.1, bf16[4096,128]{1,0:T(8,128)(2,1)} %wv_h.1, ...), custom_call_target="tpu_custom_call" | custom-call | tf_op jit(solution)/shard_map/sublayer/pallas_call | solution.py:659
  118.3 2.3 %finish.1 = (bf16[128,4096]{1,0:T(8,128)(2,1)}, f32[32,4096]{1,0:T(8,128)}) custom-call(bf16[128,4096]{1,0:T(8,128)(2,1)} %get-tuple-element.6.delta, f32[32,4096]{1,0:T(8,128)} %get-tuple-element.7.gram), custom_call_target="tpu_custom_call" | custom-call | tf_op jit(solution)/shard_map/finish/pallas_call | solution.py:670
